TPU v7x, 32 devices: a whole 2x2x4 slice. The times are simulated.
32 devices in a mesh: dp: 4 (over y, x), fsdp: 8 (over z, core).
Axes of the slice: x: 2, y: 2, z: 4, core: 2. Of those that a mesh axis runs over, the one named last changes fastest.
Arguments:
- images: bfloat16 [96, 196, 768], P(('dp', 'fsdp')), may hold values from -8 to 8
- tissue: int32 [96, 196], P(('dp', 'fsdp')), may hold values from 0 to 1, as said below
- pair_index: int32 [96], P(('dp', 'fsdp')), may hold values from 0 to 95, each once
- text_embed: bfloat16 [96, 768], P(('dp', 'fsdp')), may hold values from -0.25 to 0.25
- logit_scale: float32 [], replicated, may hold values from 30 to 80
- ln1_gain: bfloat16 [768], P(('dp', 'fsdp')), may hold values from 0.5 to 1.5
- ln1_bias: bfloat16 [768], P(('dp', 'fsdp')), may hold values from -1.25 to 1.25
- w_qkv: bfloat16 [768, 2304], P(None, ('dp', 'fsdp')), may hold values from -0.21875 to 0.21875
- bias_qv: bfloat16 [1536], P(('dp', 'fsdp')), may hold values from -1.25 to 1.25
- w_out: bfloat16 [768, 768], P(None, ('dp', 'fsdp')), may hold values from -0.625 to 0.625
- bias_out: bfloat16 [768], P(('dp', 'fsdp')), may hold values from -1.25 to 1.25
- ln2_gain: bfloat16 [768], P(('dp', 'fsdp')), may hold values from 0.5 to 1.5
- ln2_bias: bfloat16 [768], P(('dp', 'fsdp')), may hold values from -1.25 to 1.25
- w_fc1: bfloat16 [768, 3072], P(None, ('dp', 'fsdp')), may hold values from -0.21875 to 0.21875
- bias_fc1: bfloat16 [3072], P(('dp', 'fsdp')), may hold values from -1.25 to 1.25
- w_fc2: bfloat16 [3072, 768], P(('dp', 'fsdp')), may hold values from -0.15625 to 0.15625
- bias_fc2: bfloat16 [768], P(('dp', 'fsdp')), may hold values from -1.25 to 1.25
- cotangent: bfloat16 [96, 196, 768], P(('dp', 'fsdp')), may hold values from -0.0625 to 0.0625
Outputs:
- mixed_out: bfloat16 [96, 196, 768], P(('dp', 'fsdp'))
- input_grad: float32 [96, 196, 768], P(('dp', 'fsdp'))
- loss_value: float32 [], replicated
- text_grad: float32 [96, 768], P(('dp', 'fsdp'))
- grad_ln1_gain: float32 [768], P(('dp', 'fsdp'))
- grad_ln1_bias: float32 [768], P(('dp', 'fsdp'))
- grad_w_qkv: float32 [768, 2304], P(None, ('dp', 'fsdp'))
- grad_bias_qv: float32 [1536], P(('dp', 'fsdp'))
- grad_w_out: float32 [768, 768], P(None, ('dp', 'fsdp'))
- grad_bias_out: float32 [768], P(('dp', 'fsdp'))
- grad_ln2_gain: float32 [768], P(('dp', 'fsdp'))
- grad_ln2_bias: float32 [768], P(('dp', 'fsdp'))
- grad_w_fc1: float32 [768, 3072], P(None, ('dp', 'fsdp'))
- grad_bias_fc1: float32 [3072], P(('dp', 'fsdp'))
- grad_w_fc2: float32 [3072, 768], P(('dp', 'fsdp'))
- grad_bias_fc2: float32 [768], P(('dp', 'fsdp'))
Inputs may be any that keep to these rules, and one draw needn't show every extreme that they name: Every image has at least 98 tissue slots. `pair_index`: each text is paired with exactly one image.
All inputs are finite; a program needn't handle non-finite values.
Results may differ from a plain program's by a relative error of at most 0.023.
Values may be sent and summed in bfloat16 or wider, within the bound.
A program may use at most 128 MiB of HBM per device.

v0:
```python
import jax
import jax.numpy as jnp
from jax import lax
from jax.sharding import PartitionSpec as P

HEADS = 12
MICRO = 3


norm_eps = 1e-06


def layer_norm(values, gain_vec, shift_vec):
    centered = values - jnp.mean(values, -1, keepdims=True)
    variance = jnp.mean(centered * centered, -1, keepdims=True)
    return centered * lax.rsqrt(variance + norm_eps) * gain_vec + shift_vec


def unit_rows(values):
    return values * lax.rsqrt(jnp.sum(values * values, -1, keepdims=True) + norm_eps)


def exact_gelu(values):
    return jax.nn.gelu(values, approximate=False)


def split_heads(joined_qkv, image_mask):
    images_here, slot_count = image_mask.shape
    model_width = joined_qkv.shape[1] // 3
    heads_view = joined_qkv.reshape(images_here, slot_count, 3, HEADS, model_width // HEADS)
    return (heads_view[:, :, 0], heads_view[:, :, 1], heads_view[:, :, 2])


def masked_scores(queries, key_heads, image_mask):
    scores = jnp.einsum(
        "gqhd,gkhd->ghqk", queries, key_heads, preferred_element_type=jnp.float32
    ) * queries.shape[-1] ** (-0.5)
    return jnp.where(image_mask[:, None, None, :] > 0, scores, -jnp.inf)


def forward_block(params_full, token_rows, image_mask):
    (
        ln1_gain,
        ln1_bias,
        w_qkv,
        bias_qv,
        w_out,
        bias_out,
        ln2_gain,
        ln2_bias,
        w_fc1,
        bias_fc1,
        w_fc2,
        bias_fc2,
    ) = params_full
    model_width = token_rows.shape[1]
    normed = layer_norm(
        token_rows, ln1_gain.astype(jnp.float32), ln1_bias.astype(jnp.float32)
    ).astype(jnp.bfloat16)
    bias_all = jnp.concatenate(
        [bias_qv[:model_width], jnp.zeros((model_width,), jnp.bfloat16), bias_qv[model_width:]]
    ).astype(jnp.float32)
    joined_qkv = (jnp.dot(normed, w_qkv, preferred_element_type=jnp.float32) + bias_all).astype(
        jnp.bfloat16
    )
    queries, key_heads, values = split_heads(joined_qkv, image_mask)
    scores = masked_scores(queries, key_heads, image_mask)
    row_top = jnp.max(scores, -1, keepdims=True)
    exp_terms = jnp.exp(scores - row_top)
    row_total = jnp.sum(exp_terms, -1, keepdims=True)
    attn_probs = (exp_terms / row_total).astype(jnp.bfloat16)
    log_total = row_top + jnp.log(row_total)
    attended = jnp.einsum("ghqk,gkhd->gqhd", attn_probs, values, preferred_element_type=jnp.float32)
    attended = attended.reshape(-1, model_width).astype(jnp.bfloat16)
    hidden = (
        token_rows
        + jnp.dot(attended, w_out, preferred_element_type=jnp.float32)
        + bias_out.astype(jnp.float32)
    )
    second = layer_norm(hidden, ln2_gain.astype(jnp.float32), ln2_bias.astype(jnp.float32)).astype(
        jnp.bfloat16
    )
    pre_act = jnp.dot(second, w_fc1, preferred_element_type=jnp.float32) + bias_fc1.astype(
        jnp.float32
    )
    activated = exact_gelu(pre_act).astype(jnp.bfloat16)
    outputs = (
        hidden
        + jnp.dot(activated, w_fc2, preferred_element_type=jnp.float32)
        + bias_fc2.astype(jnp.float32)
    ) * image_mask.reshape(-1, 1)
    saved_state = (normed, joined_qkv, log_total, attended, hidden, second, pre_act, activated)
    return (outputs, saved_state)


def backward_block(params_full, token_rows, image_mask, saved_state, grad_out):
    (
        ln1_gain,
        ln1_bias,
        w_qkv,
        bias_qv,
        w_out,
        bias_out,
        ln2_gain,
        ln2_bias,
        w_fc1,
        bias_fc1,
        w_fc2,
        bias_fc2,
    ) = params_full
    normed, joined_qkv, log_total, attended, hidden, second, pre_act, activated = saved_state
    model_width = token_rows.shape[1]
    grad_branch2 = grad_out.astype(jnp.bfloat16)
    grad_w_fc2 = jnp.einsum(
        "nf,nd->fd", activated, grad_branch2, preferred_element_type=jnp.float32
    )
    grad_bias_fc2 = jnp.sum(grad_branch2.astype(jnp.float32), 0)
    grad_act = jnp.einsum("nd,fd->nf", grad_branch2, w_fc2, preferred_element_type=jnp.float32)
    gelu_value, gelu_pull = jax.vjp(exact_gelu, pre_act)
    grad_pre = gelu_pull(grad_act)[0].astype(jnp.bfloat16)
    grad_w_fc1 = jnp.einsum("nd,nf->df", second, grad_pre, preferred_element_type=jnp.float32)
    grad_bias_fc1 = jnp.sum(grad_pre.astype(jnp.float32), 0)
    grad_second = jnp.einsum("nf,df->nd", grad_pre, w_fc1, preferred_element_type=jnp.float32)
    norm_value, norm_pull = jax.vjp(
        layer_norm, hidden, ln2_gain.astype(jnp.float32), ln2_bias.astype(jnp.float32)
    )
    grad_hidden_norm, grad_ln2_gain, grad_ln2_bias = norm_pull(grad_second)
    grad_hidden = grad_out + grad_hidden_norm
    grad_branch1 = grad_hidden.astype(jnp.bfloat16)
    grad_w_out = jnp.einsum("nd,ne->de", attended, grad_branch1, preferred_element_type=jnp.float32)
    grad_bias_out = jnp.sum(grad_branch1.astype(jnp.float32), 0)
    grad_attended = jnp.einsum(
        "ne,de->nd", grad_branch1, w_out, preferred_element_type=jnp.float32
    ).astype(jnp.bfloat16)
    queries, key_heads, values = split_heads(joined_qkv, image_mask)
    grad_attended = grad_attended.reshape(values.shape)
    scores = masked_scores(queries, key_heads, image_mask)
    attn_probs = jnp.exp(scores - log_total)
    grad_values = jnp.einsum(
        "ghqk,gqhd->gkhd",
        attn_probs.astype(jnp.bfloat16),
        grad_attended,
        preferred_element_type=jnp.float32,
    )
    grad_probs = jnp.einsum(
        "gqhd,gkhd->ghqk", grad_attended, values, preferred_element_type=jnp.float32
    )
    inner_sum = jnp.sum(grad_probs * attn_probs, -1, keepdims=True)
    grad_scores = (attn_probs * (grad_probs - inner_sum)).astype(jnp.bfloat16)
    head_scale = queries.shape[-1] ** (-0.5)
    grad_queries = (
        jnp.einsum("ghqk,gkhd->gqhd", grad_scores, key_heads, preferred_element_type=jnp.float32)
        * head_scale
    )
    grad_keys = (
        jnp.einsum("ghqk,gqhd->gkhd", grad_scores, queries, preferred_element_type=jnp.float32)
        * head_scale
    )
    grad_joined = (
        jnp.stack([grad_queries, grad_keys, grad_values], 2)
        .reshape(-1, 3 * model_width)
        .astype(jnp.bfloat16)
    )
    grad_w_qkv = jnp.einsum("nd,nf->df", normed, grad_joined, preferred_element_type=jnp.float32)
    joined_sums = jnp.sum(grad_joined.astype(jnp.float32), 0)
    grad_bias_qv = jnp.concatenate([joined_sums[:model_width], joined_sums[2 * model_width :]])
    grad_normed = jnp.einsum("nf,df->nd", grad_joined, w_qkv, preferred_element_type=jnp.float32)
    first_value, first_pull = jax.vjp(
        layer_norm, token_rows, ln1_gain.astype(jnp.float32), ln1_bias.astype(jnp.float32)
    )
    grad_rows, grad_ln1_gain, grad_ln1_bias = first_pull(grad_normed)
    grad_input = grad_hidden + grad_rows
    grad_list = (
        grad_ln1_gain,
        grad_ln1_bias,
        grad_w_qkv,
        grad_bias_qv,
        grad_w_out,
        grad_bias_out,
        grad_ln2_gain,
        grad_ln2_bias,
        grad_w_fc1,
        grad_bias_fc1,
        grad_w_fc2,
        grad_bias_fc2,
    )
    return (grad_input, grad_list)


def per_device(
    images,
    tissue,
    pair_index,
    text_embed,
    logit_scale,
    ln1_gain,
    ln1_bias,
    w_qkv,
    bias_qv,
    w_out,
    bias_out,
    ln2_gain,
    ln2_bias,
    w_fc1,
    bias_fc1,
    w_fc2,
    bias_fc2,
    cotangent,
):
    local_images, slot_count, model_width = images.shape
    per_micro = local_images // MICRO
    tissue_float = tissue.astype(jnp.float32)
    saved_all = []
    pooled_parts = []
    mixed_parts = []
    for micro_step in range(MICRO):
        params_full = (
            lax.all_gather(ln1_gain, ("dp", "fsdp"), axis=0, tiled=True),
            lax.all_gather(ln1_bias, ("dp", "fsdp"), axis=0, tiled=True),
            lax.all_gather(w_qkv, ("dp", "fsdp"), axis=1, tiled=True),
            lax.all_gather(bias_qv, ("dp", "fsdp"), axis=0, tiled=True),
            lax.all_gather(w_out, ("dp", "fsdp"), axis=1, tiled=True),
            lax.all_gather(bias_out, ("dp", "fsdp"), axis=0, tiled=True),
            lax.all_gather(ln2_gain, ("dp", "fsdp"), axis=0, tiled=True),
            lax.all_gather(ln2_bias, ("dp", "fsdp"), axis=0, tiled=True),
            lax.all_gather(w_fc1, ("dp", "fsdp"), axis=1, tiled=True),
            lax.all_gather(bias_fc1, ("dp", "fsdp"), axis=0, tiled=True),
            lax.all_gather(w_fc2, ("dp", "fsdp"), axis=0, tiled=True),
            lax.all_gather(bias_fc2, ("dp", "fsdp"), axis=0, tiled=True),
        )
        first_image = micro_step * per_micro
        token_rows = (
            images[first_image : first_image + per_micro]
            .reshape(-1, model_width)
            .astype(jnp.float32)
        )
        image_mask = tissue_float[first_image : first_image + per_micro]
        outputs, saved_state = forward_block(params_full, token_rows, image_mask)
        saved_all.append(saved_state)
        shaped = outputs.reshape(per_micro, slot_count, model_width)
        mixed_parts.append(shaped.astype(jnp.bfloat16))
        pooled_parts.append(jnp.sum(shaped, 1))
    mixed_out = jnp.concatenate(mixed_parts, 0)
    counts = jnp.sum(tissue_float, 1)[:, None]
    pooled = jnp.concatenate(pooled_parts, 0) / counts
    text_float = text_embed.astype(jnp.float32)
    text_unit = unit_rows(text_float).astype(jnp.bfloat16)
    image_float, unit_pull = jax.vjp(unit_rows, pooled)
    image_unit = image_float.astype(jnp.bfloat16)
    all_texts, all_images = (
        lax.all_gather(text_unit, ("dp", "fsdp"), axis=0, tiled=True),
        lax.all_gather(image_unit, ("dp", "fsdp"), axis=0, tiled=True),
    )
    all_pairs = lax.all_gather(pair_index, ("dp", "fsdp"), axis=0, tiled=True)
    total_texts = all_texts.shape[0]
    own_start = lax.axis_index(("dp", "fsdp")) * local_images
    logits = logit_scale * jnp.einsum(
        "id,jd->ij", image_unit, all_texts, preferred_element_type=jnp.float32
    )
    col_logits = logit_scale * jnp.einsum(
        "id,jd->ij", all_images, text_unit, preferred_element_type=jnp.float32
    )
    row_top = jnp.max(logits, 1, keepdims=True)
    row_lse = row_top[:, 0] + jnp.log(jnp.sum(jnp.exp(logits - row_top), 1))
    col_top = jnp.max(col_logits, 0, keepdims=True)
    col_lse = col_top[0] + jnp.log(jnp.sum(jnp.exp(col_logits - col_top), 0))
    pair_match = (lax.broadcasted_iota(jnp.int32, logits.shape, 1) == pair_index[:, None]).astype(
        jnp.float32
    )
    paired_terms = jnp.sum(logits * pair_match, 1)
    all_row_lse, all_col_lse, all_paired = (
        lax.all_gather(row_lse, ("dp", "fsdp"), axis=0, tiled=True),
        lax.all_gather(col_lse, ("dp", "fsdp"), axis=0, tiled=True),
        lax.all_gather(paired_terms, ("dp", "fsdp"), axis=0, tiled=True),
    )
    loss_value = (jnp.sum(all_row_lse) + jnp.sum(all_col_lse) - 2.0 * jnp.sum(all_paired)) / (
        2.0 * total_texts
    )
    row_grad = (
        0.5 * (jnp.exp(logits - row_lse[:, None]) + jnp.exp(logits - all_col_lse[None, :]))
        - pair_match
    )
    grad_raw = (logit_scale * row_grad).astype(jnp.bfloat16)
    grad_unit = jnp.einsum("ij,jd->id", grad_raw, all_texts, preferred_element_type=jnp.float32)
    own_columns = lax.broadcasted_iota(jnp.int32, col_logits.shape, 1) + own_start
    col_match = (own_columns == all_pairs[:, None]).astype(jnp.float32)
    col_grad = (
        0.5 * (jnp.exp(col_logits - all_row_lse[:, None]) + jnp.exp(col_logits - col_lse[None, :]))
        - col_match
    )
    col_raw = (logit_scale * col_grad).astype(jnp.bfloat16)
    grad_text_unit = jnp.einsum(
        "ij,id->jd", col_raw, all_images, preferred_element_type=jnp.float32
    )
    text_value, text_pull = jax.vjp(unit_rows, text_float)
    text_grad = text_pull(grad_text_unit)[0]
    grad_pooled = unit_pull(grad_unit)[0] / counts
    grad_totals = None
    input_parts = []
    for micro_step in range(MICRO):
        params_full = (
            lax.all_gather(ln1_gain, ("dp", "fsdp"), axis=0, tiled=True),
            lax.all_gather(ln1_bias, ("dp", "fsdp"), axis=0, tiled=True),
            lax.all_gather(w_qkv, ("dp", "fsdp"), axis=1, tiled=True),
            lax.all_gather(bias_qv, ("dp", "fsdp"), axis=0, tiled=True),
            lax.all_gather(w_out, ("dp", "fsdp"), axis=1, tiled=True),
            lax.all_gather(bias_out, ("dp", "fsdp"), axis=0, tiled=True),
            lax.all_gather(ln2_gain, ("dp", "fsdp"), axis=0, tiled=True),
            lax.all_gather(ln2_bias, ("dp", "fsdp"), axis=0, tiled=True),
            lax.all_gather(w_fc1, ("dp", "fsdp"), axis=1, tiled=True),
            lax.all_gather(bias_fc1, ("dp", "fsdp"), axis=0, tiled=True),
            lax.all_gather(w_fc2, ("dp", "fsdp"), axis=0, tiled=True),
            lax.all_gather(bias_fc2, ("dp", "fsdp"), axis=0, tiled=True),
        )
        first_image = micro_step * per_micro
        token_rows = (
            images[first_image : first_image + per_micro]
            .reshape(-1, model_width)
            .astype(jnp.float32)
        )
        image_mask = tissue_float[first_image : first_image + per_micro]
        grad_block = (
            cotangent[first_image : first_image + per_micro].astype(jnp.float32)
            + grad_pooled[first_image : first_image + per_micro][:, None, :]
        ) * image_mask[:, :, None]
        grad_input, grad_list = backward_block(
            params_full,
            token_rows,
            image_mask,
            saved_all[micro_step],
            grad_block.reshape(-1, model_width),
        )
        input_parts.append(grad_input.reshape(per_micro, slot_count, model_width))
        if grad_totals is None:
            grad_totals = grad_list
        else:
            grad_totals = jax.tree.map(jnp.add, grad_totals, grad_list)
    shares = (
        lax.psum_scatter(grad_totals[0], ("dp", "fsdp"), scatter_dimension=0, tiled=True),
        lax.psum_scatter(grad_totals[1], ("dp", "fsdp"), scatter_dimension=0, tiled=True),
        lax.psum_scatter(grad_totals[2], ("dp", "fsdp"), scatter_dimension=1, tiled=True),
        lax.psum_scatter(grad_totals[3], ("dp", "fsdp"), scatter_dimension=0, tiled=True),
        lax.psum_scatter(grad_totals[4], ("dp", "fsdp"), scatter_dimension=1, tiled=True),
        lax.psum_scatter(grad_totals[5], ("dp", "fsdp"), scatter_dimension=0, tiled=True),
        lax.psum_scatter(grad_totals[6], ("dp", "fsdp"), scatter_dimension=0, tiled=True),
        lax.psum_scatter(grad_totals[7], ("dp", "fsdp"), scatter_dimension=0, tiled=True),
        lax.psum_scatter(grad_totals[8], ("dp", "fsdp"), scatter_dimension=1, tiled=True),
        lax.psum_scatter(grad_totals[9], ("dp", "fsdp"), scatter_dimension=0, tiled=True),
        lax.psum_scatter(grad_totals[10], ("dp", "fsdp"), scatter_dimension=0, tiled=True),
        lax.psum_scatter(grad_totals[11], ("dp", "fsdp"), scatter_dimension=0, tiled=True),
    )
    input_grad = jnp.concatenate(input_parts, 0)
    return (
        mixed_out,
        input_grad,
        loss_value,
        text_grad,
        shares[0],
        shares[1],
        shares[2],
        shares[3],
        shares[4],
        shares[5],
        shares[6],
        shares[7],
        shares[8],
        shares[9],
        shares[10],
        shares[11],
    )


def solution(mesh):
    in_specs = (
        P(("dp", "fsdp"), None, None),
        P(("dp", "fsdp"), None),
        P(("dp", "fsdp")),
        P(("dp", "fsdp"), None),
        P(),
        P(("dp", "fsdp")),
        P(("dp", "fsdp")),
        P(None, ("dp", "fsdp")),
        P(("dp", "fsdp")),
        P(None, ("dp", "fsdp")),
        P(("dp", "fsdp")),
        P(("dp", "fsdp")),
        P(("dp", "fsdp")),
        P(None, ("dp", "fsdp")),
        P(("dp", "fsdp")),
        P(("dp", "fsdp"), None),
        P(("dp", "fsdp")),
        P(("dp", "fsdp"), None, None),
    )
    out_specs = (
        P(("dp", "fsdp"), None, None),
        P(("dp", "fsdp"), None, None),
        P(),
        P(("dp", "fsdp"), None),
        P(("dp", "fsdp")),
        P(("dp", "fsdp")),
        P(None, ("dp", "fsdp")),
        P(("dp", "fsdp")),
        P(None, ("dp", "fsdp")),
        P(("dp", "fsdp")),
        P(("dp", "fsdp")),
        P(("dp", "fsdp")),
        P(None, ("dp", "fsdp")),
        P(("dp", "fsdp")),
        P(("dp", "fsdp"), None),
        P(("dp", "fsdp")),
    )
    return jax.shard_map(
        per_device, mesh=mesh, in_specs=in_specs, out_specs=out_specs, check_vma=False
    )
```

profile of v0, /device:TPU:0, one launch (start us, length us, event | category | flops | bytes accessed | tf_op | source)
XLA Modules:
  0.0 956.0 jit_solution(3620799874080125043)
XLA Ops:
  10.0 1.3 convert_reduce_fusion.15
  13.5 1.4 convert_reduce_fusion.8
  14.9 1.6 fusion.82
  25.2 42.9 %all-reduce.21 = (bf16[1536]{0:T(1024)(128)(2,1)S(1)}, bf16[768]{0:T(1024)(128)(2,1)S(1)}, bf16[768]{0:T(1024)(128)(2,1)S(1)}, bf16[768]{0:T(1024)(128)(2,1)S(1)...) all-reduce(bf16[1536]{0:T(1024)(128)(2,1)S(1)} %dynamic-update-slic, ...), channel_id=1, replica_groups=mesh['dp'=4,'fsdp'=8] {'dp','fsdp'}, use_global_device_ids=true, to_apply=%add.2 | all-reduce | flops 9216 | bytes 36864
  68.1 41.3 %all-gather = bf16[32,3,768]{2,1,0:T(4,128)(2,1)S(1)} all-gather(bf16[1,3,768]{2,1,0:T(4,128)(2,1)S(1)} %fusion.170), channel_id=1, replica_groups=mesh['dp'=4,'fsdp'=8] {'dp','fsdp'}, dimensions={0}, use_global_device_ids=true | all-gather | bytes 152064 | tf_op jit(solution)/shard_map/all_gather | solution.py:251
  110.2 3.3 fusion.1
  113.5 1.4 copy.81
  115.0 3.3 fusion.2
  118.3 1.5 copy.83
  119.8 3.3 fusion
  126.5 4.1 all-gather.9.cloned.1.call-done
  130.6 2.0 fusion.206
  141.3 55.0 %all-gather.11.cloned.1.call-done = bf16[768,3072]{0,1:T(8,128)(2,1)} async-done(((bf16[768,96]{0,1:T(8,128)(2,1)}), bf16[768,3072]{0,1:T(8,128)(2,1)}) %all-gather.11.cloned.1.call-update) | async-done | bytes 4718608 | tf_op jit(solution)/shard_map/all_gather | solution.py:226
  196.3 10.3 %multiply_convert_fusion.3 = (bf16[196,3072]{1,0:T(8,128)(2,1)}, f32[196,3072]{1,0:T(8,128)}, f32[196,3072]{1,0:T(8,128)}) fusion(f32[3072]{0:T(1024)S(1)} %convert_element_type.427, bf16[768,3072]{0,1:T(8,128)(2,1)} %all-gather.11.cloned.1.call-done, f32[196,768]{1,0:T(8,128)} %copy-done.13, f32[196]{0:T(256)S(1)} %fusion.166, ...), kind=kOutput, calls=%fused_computation.33 | convolution fusion | flops 965336064 | bytes 11361824 | tf_op jit(solution)/shard_map/dot_general | solution.py:83
  206.6 55.1 %all-gather.13.cloned.1.call-done = bf16[3072,768]{1,0:T(8,128)(2,1)} async-done(((bf16[96,768]{1,0:T(8,128)(2,1)}), bf16[3072,768]{1,0:T(8,128)(2,1)}) %all-gather.13.cloned.1.call-update) | async-done | bytes 4718608 | tf_op jit(solution)/shard_map/all_gather | solution.py:228
  261.7 4.9 fusion.195
  266.6 8.0 multiply_convert_fusion.4
  274.6 8.0 multiply_convert_fusion.5
  283.9 2.0 fusion.193
  286.2 42.8 %all-gather.1 = bf16[32,3,768]{2,1,0:T(4,128)(2,1)} all-gather(bf16[1,3,768]{2,1,0:T(4,128)(2,1)S(1)} %fusion.171), channel_id=1, replica_groups=mesh['dp'=4,'fsdp'=8] {'dp','fsdp'}, dimensions={0}, use_global_device_ids=true | all-gather | bytes 152064 | tf_op jit(solution)/shard_map/all_gather | solution.py:252
  329.0 1.7 reshape.985
  330.7 1.2 fusion.208
  332.0 1.2 fusion.207
  334.5 37.1 %all-reduce.8 = f32[96]{0:T(128)} all-reduce(f32[96]{0:T(128)} %copy-done.128), channel_id=1, replica_groups=mesh['dp'=4,'fsdp'=8] {'dp','fsdp'}, use_global_device_ids=true, to_apply=%add.8 | all-reduce | flops 96 | bytes 768
  371.5 1.4 select_reduce_fusion
  373.7 1.2 multiply_reduce_fusion.12
  376.4 6.6 convert_reduce_fusion.1
  383.0 4.0 fusion.209
  387.1 5.6 convert_reduce_fusion
  395.6 2.7 convert_reduce_fusion.2
  398.3 2.1 multiply_reduce_fusion.5
  401.4 2.1 convert_reduce_fusion.10
  403.5 1.9 fusion.212
  406.6 1.9 copy.85
  408.5 3.2 convolution_bitcast_fusion.2
  411.7 1.7 multiply_reduce_fusion.2
  414.7 1.3 fusion.31
  417.0 1.9 fusion.213
  420.1 1.9 copy.89
  422.1 3.3 convolution_bitcast_fusion.1
  425.3 1.7 multiply_reduce_fusion.1
  428.3 1.3 fusion.29
  431.9 1.9 copy.93
  433.8 4.6 add_add_fusion.3
  438.4 1.8 convert_reduce_fusion.5
  440.2 1.7 convert_reduce_fusion.4
  447.5 4.3 add_add_fusion.2
  453.3 1.6 fusion.181
  455.0 1.6 fusion.180
  456.6 5.3 add_add_fusion.1
  463.5 1.5 fusion.174
  465.0 1.5 fusion.172
  466.6 5.3 add_add_fusion
  472.7 42.7 %all-reduce.11 = s32[96]{0:T(128)} all-reduce(s32[96]{0:T(128)S(1)} %dynamic-update-slice.11), channel_id=1, replica_groups=mesh['dp'=4,'fsdp'=8] {'dp','fsdp'}, use_global_device_ids=true, to_apply=%add.11 | all-reduce | flops 96 | bytes 768
  517.2 3.1 fusion.211
  522.1 1.9 fusion.77
  524.3 1.5 fusion.71
  525.9 39.9 %all-reduce.20 = (f32[96]{0:T(128)S(1)}, f32[96]{0:T(128)S(1)}, f32[768]{0:T(1024)S(1)}, f32[768]{0:T(1024)S(1)}, f32[1536]{0:T(1024)S(1)}, /*index=5*/f32[768]{...) all-reduce(f32[96]{0:T(128)} %copy-done.117, ...), channel_id=1, replica_groups=mesh['dp'=4,'fsdp'=8] {'dp','fsdp'}, use_global_device_ids=true, to_apply=%add.9 | all-reduce | flops 9408 | bytes 75264
  573.6 2.2 pad_maximum_fusion.1
  575.8 1.5 add_bitcast_fusion.2
  577.8 1.4 pad_maximum_fusion
  580.3 84.0 %reduce-scatter.5.cloned.1.call-done = f32[768,72]{0,1:T(8,128)} async-done(((f32[768,2304]{0,1:T(8,128)}), f32[768,72]{0,1:T(8,128)}) %reduce-scatter.5.cloned.1.call-update) | async-done | bytes 221200 | tf_op jit(solution)/shard_map/reduce_scatter | solution.py:341
  664.3 141.6 %reduce-scatter.9.cloned.1.call-done = f32[768,96]{0,1:T(8,128)} async-done(((f32[768,3072]{0,1:T(8,128)}), f32[768,96]{0,1:T(8,128)}) %reduce-scatter.9.cloned.1.call-update) | async-done | bytes 294928 | tf_op jit(solution)/shard_map/reduce_scatter | solution.py:347
  805.9 142.0 %reduce-scatter.11.cloned.1.call-done = f32[96,768]{1,0:T(8,128)} async-done(((f32[3072,768]{1,0:T(8,128)}), f32[96,768]{1,0:T(8,128)}) %reduce-scatter.11.cloned.1.call-update) | async-done | bytes 294928 | tf_op jit(solution)/shard_map/reduce_scatter | solution.py:349
  (452 shorter events, 62.6 us)
Async XLA Ops:
  7.2 103.0 %copy-start.8 = (bf16[3,196,768]{2,1,0:T(8,128)(2,1)S(1)}, bf16[3,196,768]{2,1,0:T(8,128)(2,1)}, u32[]{:S(2)}) copy-start(bf16[3,196,768]{2,1,0:T(8,128)(2,1)} %param.18) | copy-start | bytes 2709508
  7.2 103.0 %all-gather.7.cloned.1.call-start = ((), (), s32[]{:S(2)}) async-start(), calls=%async_computation.4 | async-start | bytes 3649536 | tf_op jit(solution)/shard_map/all_gather | solution.py:220
  7.9 122.7 %all-gather.9.cloned.1.call-start = ((), (), s32[]{:S(2)}) async-start(), calls=%async_computation.5 | async-start | bytes 1216512 | tf_op jit(solution)/shard_map/all_gather | solution.py:222
  8.7 187.7 %all-gather.11.cloned.1.call-start = ((), (), s32[]{:S(2)}) async-start(), calls=%async_computation.6 | async-start | bytes 4866048 | tf_op jit(solution)/shard_map/all_gather | solution.py:226
  9.4 252.3 %all-gather.13.cloned.1.call-start = ((), (), s32[]{:S(2)}) async-start(), calls=%async_computation.7 | async-start | bytes 4866048 | tf_op jit(solution)/shard_map/all_gather | solution.py:228
  10.0 570.3 %reduce-scatter.7.cloned.1.call-start = ((), (), s32[]{:S(2)}) async-start(), calls=%async_computation.9 | async-start | bytes 2433024 | tf_op jit(solution)/shard_map/reduce_scatter | solution.py:343
  13.5 4.1 copy-start.122
  13.5 8.2 copy-start.110
  16.5 6.1 copy-start.99
  16.5 98.4 %copy-start.86 = (f32[196]{0:T(256)}, f32[196]{0:T(256)S(1)}, u32[]{:S(2)}) copy-start(f32[196]{0:T(256)S(1)} %fusion.165) | copy-start | bytes 2356
  17.1 96.4 %copy-start.80 = (f32[196]{0:T(256)}, f32[196]{0:T(256)S(1)}, u32[]{:S(2)}) copy-start(f32[196]{0:T(256)S(1)} %fusion.163) | copy-start | bytes 2356
  126.5 6.4 copy-start.52
  141.2 65.5 %copy-start.101 = (f32[196]{0:T(256)}, f32[196]{0:T(256)S(1)}, u32[]{:S(2)}) copy-start(f32[196]{0:T(256)S(1)} %multiply_reduce_fusion.10) | copy-start | bytes 2356
  141.2 259.3 %copy-start.76 = (f32[196]{0:T(256)}, f32[196]{0:T(256)S(1)}, u32[]{:S(2)}) copy-start(f32[196]{0:T(256)S(1)} %fusion.162) | copy-start | bytes 2356
  141.2 259.3 %copy-start.74 = (f32[196]{0:T(256)}, f32[196]{0:T(256)S(1)}, u32[]{:S(2)}) copy-start(f32[196]{0:T(256)S(1)} %fusion.166) | copy-start | bytes 2356
  141.2 259.3 %copy-start.78 = (f32[196]{0:T(256)}, f32[196]{0:T(256)S(1)}, u32[]{:S(2)}) copy-start(f32[196]{0:T(256)S(1)} %fusion.164) | copy-start | bytes 2356
  261.7 4.9 copy-start.10
  261.7 4.9 copy-start.126
  266.6 8.0 copy-start.17
  266.6 16.1 %slice-start = ((s8[4718592]{0:T(1024)(128)(4,1)}), s8[4194304]{0:T(1024)(128)(4,1)S(1)}, s32[]{:S(2)}) async-start(s8[4718592]{0:T(1024)(128)(4,1)} %bitcast.400), calls=%async_computation.12 | async-start | bytes 8388608
  274.6 9.2 copy-start.28
  274.6 8.0 slice-start.1
  283.9 48.0 %copy-start.69 = (bf16[3,768]{1,0:T(4,128)(2,1)S(1)}, bf16[3,768]{1,0:T(4,128)(2,1)}, u32[]{:S(2)}) copy-start(bf16[3,768]{1,0:T(4,128)(2,1)} %param.21) | copy-start | bytes 13828
  283.9 48.0 %copy-start.111 = (f32[3]{0:T(128)S(1)}, f32[3]{0:T(128)}, u32[]{:S(2)}) copy-start(f32[3]{0:T(128)} %copy-done.110) | copy-start | bytes 40
  286.1 44.6 %copy-start.120 = (f32[3]{0:T(128)}, f32[3]{0:T(128)S(1)}, u32[]{:S(2)}) copy-start(f32[3]{0:T(128)S(1)} %get-tuple-element.93) | copy-start | bytes 40
  286.2 89.4 %copy-start.113 = (f32[3]{0:T(128)}, f32[3]{0:T(128)S(1)}, u32[]{:S(2)}) copy-start(f32[3]{0:T(128)S(1)} %add_rsqrt_fusion.1) | copy-start | bytes 40
  333.2 42.4 %copy-start.114 = (f32[96,3]{0,1:T(4,128)}, f32[96,3]{0,1:T(4,128)S(1)}, u32[]{:S(2)}) copy-start(f32[96,3]{0,1:T(4,128)S(1)} %get-tuple-element.151) | copy-start | bytes 3460
  376.4 10.7 %copy-start.132 = (f32[196,3072]{1,0:T(8,128)S(1)}, f32[196,3072]{1,0:T(8,128)}, u32[]{:S(2)}) copy-start(f32[196,3072]{1,0:T(8,128)} %get-tuple-element.100) | copy-start | bytes 7225348
  376.4 10.7 %copy-start.133 = (f32[196,3072]{1,0:T(8,128)S(1)}, f32[196,3072]{1,0:T(8,128)}, u32[]{:S(2)}) copy-start(f32[196,3072]{1,0:T(8,128)} %get-tuple-element.139) | copy-start | bytes 7225348
  383.0 4.0 copy-start.60
  383.0 4.0 copy-start.26
  383.0 9.7 %slice-start.4 = ((s8[4718592]{0:T(1024)(128)(4,1)}), s8[4194304]{0:T(1024)(128)(4,1)S(1)}, s32[]{:S(2)}) async-start(s8[4718592]{0:T(1024)(128)(4,1)} %bitcast.438), calls=%async_computation.16 | async-start | bytes 8388608
  383.0 10.9 %slice-start.2 = ((s8[4718592]{0:T(1024)(128)(4,1)}), s8[4194304]{0:T(1024)(128)(4,1)S(1)}, s32[]{:S(2)}) async-start(s8[4718592]{0:T(1024)(128)(4,1)} %bitcast.402), calls=%async_computation.14 | async-start | bytes 8388608
  387.1 5.6 slice-start.5
  387.1 6.9 slice-start.3
  401.3 4.1 copy-start.30
  401.3 4.1 copy-start.32
  401.3 4.1 copy-start.34
  401.3 4.1 copy-start.91
  401.4 4.1 copy-start.89
  401.4 4.0 copy-start.93
  408.5 3.2 copy-start.1
  408.5 3.2 copy-start.43
  422.0 3.3 copy-start.3
  422.1 3.3 copy-start.44
  438.3 226.0 %reduce-scatter.5.cloned.1.call-start = ((), (), s32[]{:S(2)}) async-start(), calls=%async_computation.8 | async-start | bytes 7299072 | tf_op jit(solution)/shard_map/reduce_scatter | solution.py:341
  438.4 3.5 copy-start.21
  438.4 3.5 copy-start.42
  440.2 6.0 copy-start.38
  451.8 354.0 %reduce-scatter.9.cloned.1.call-start = ((), (), s32[]{:S(2)}) async-start(), calls=%async_computation.10 | async-start | bytes 9732096 | tf_op jit(solution)/shard_map/reduce_scatter | solution.py:347
  461.9 486.0 %reduce-scatter.11.cloned.1.call-start = ((), (), s32[]{:S(2)}) async-start(), calls=%async_computation.11 | async-start | bytes 9732096 | tf_op jit(solution)/shard_map/reduce_scatter | solution.py:349
  471.9 44.1 %copy-start.129 = (f32[96]{0:T(128)S(1)}, f32[96]{0:T(128)}, u32[]{:S(2)}) copy-start(f32[96]{0:T(128)} %all-reduce.8) | copy-start | bytes 1156
  471.9 45.1 %copy-start.124 = (f32[3]{0:T(128)S(1)}, f32[3]{0:T(128)}, u32[]{:S(2)}) copy-start(f32[3]{0:T(128)} %get-tuple-element.51) | copy-start | bytes 40
  471.9 45.3 %copy-start.37 = (bf16[1,196,3,12,64]{1,4,3,2,0:T(8,128)(2,1)S(1)}, bf16[1,196,3,12,64]{1,4,3,2,0:T(8,128)(2,1)}, u32[]{:S(2)}) copy-start(bf16[1,196,3,12,64]{1,4,3,2,0:T(8,128)(2,1)} %copy-done.36) | copy-start | bytes 2709508
  517.2 3.2 copy-start.118
  517.2 3.1 copy-start.41
  517.2 3.5 copy-start.127
  524.1 49.6 %copy-start.64 = (bf16[1,196,768]{2,1,0:T(8,128)(2,1)S(1)}, bf16[1,196,768]{2,1,0:T(8,128)(2,1)}, u32[]{:S(2)}) copy-start(bf16[1,196,768]{2,1,0:T(8,128)(2,1)} %get-tuple-element.109) | copy-start | bytes 903172
  524.3 51.5 %copy-start.116 = (f32[196]{0:T(256)S(1)}, f32[196]{0:T(256)}, u32[]{:S(2)}) copy-start(f32[196]{0:T(256)} %get-tuple-element.28) | copy-start | bytes 2356
  524.3 51.5 %copy-start.33 = (f32[196,768]{1,0:T(8,128)S(1)}, f32[196,768]{1,0:T(8,128)}, u32[]{:S(2)}) copy-start(f32[196,768]{1,0:T(8,128)} %copy-done.32) | copy-start | bytes 1806340
  524.3 51.5 %copy-start.92 = (f32[196]{0:T(256)S(1)}, f32[196]{0:T(256)}, u32[]{:S(2)}) copy-start(f32[196]{0:T(256)} %copy-done.91) | copy-start | bytes 2356
  525.8 51.5 %copy-start.31 = (f32[196,768]{1,0:T(8,128)S(1)}, f32[196,768]{1,0:T(8,128)}, u32[]{:S(2)}) copy-start(f32[196,768]{1,0:T(8,128)} %copy-done.30) | copy-start | bytes 1806340
  525.8 51.5 %copy-start.90 = (f32[196]{0:T(256)S(1)}, f32[196]{0:T(256)}, u32[]{:S(2)}) copy-start(f32[196]{0:T(256)} %copy-done.89) | copy-start | bytes 2356
  573.6 3.8 copy-start.67
  (86 other events, 153.9 us)
Sparse Core Ops, SparseCore 0:
  11.0 63.5 all-gather.6
  77.6 52.9 all-gather.8
  133.7 62.5 all-gather.10
  199.2 62.4 all-gather.12
  438.4 100.7 reduce-scatter.6
  546.3 118.0 reduce-scatter.4
  670.8 135.0 reduce-scatter.8
  813.4 134.4 reduce-scatter.10
where the time goes:
time: 961 us; the launch traced here: 956 us
  waiting for transfers between devices  484 us (50%)
  blocking collectives  247 us (26%)
  matrix products  136 us (14%)
  local copies, waits for them, and re-layouts  36.5 us (4%)
  other arithmetic  31.5 us (3%)
  between operations  20.1 us (2%)
    unnamed x4, blocking collectives  162 us
    reduce_scatter x1, waiting for transfers between devices, per_device(): lax.psum_scatter(grad_totals[10], ('dp', 'fsdp'), scatter_dimension=0, ti...  142 us
    reduce_scatter x1, waiting for transfers between devices, per_device(): lax.psum_scatter(grad_totals[8], ('dp', 'fsdp'), scatter_dimension=1, til...  142 us
    reduce_scatter x1, waiting for transfers between devices, per_device(): lax.psum_scatter(grad_totals[2], ('dp', 'fsdp'), scatter_dimension=1, til...  84 us
    all_gather x1, waiting for transfers between devices, per_device(): lax.all_gather(w_fc2, ('dp', 'fsdp'), axis=0, tiled=True)  55.1 us
    all_gather x1, waiting for transfers between devices, per_device(): lax.all_gather(w_fc1, ('dp', 'fsdp'), axis=1, tiled=True)  55 us
    all_gather x1, blocking collectives, per_device(): lax.all_gather(image_unit, ('dp', 'fsdp'), axis=0, tiled=True)  42.8 us
    all_gather x1, blocking collectives, per_device(): lax.all_gather(text_unit, ('dp', 'fsdp'), axis=0, tiled=True)  41.3 us
  transfers between devices with their start and end apart: 8, of which 6 were waited for; matrix products, arithmetic and copies ran while one was open for 10% of the time, Pallas kernels for 0%

commit v1 on v0

--- a/solution.py
+++ b/solution.py
@@ -1,11 +1,284 @@
+import functools
 import jax
 import jax.numpy as jnp
 from jax import lax
+from jax.experimental import pallas as pl
+from jax.experimental.pallas import tpu as pltpu
 from jax.sharding import PartitionSpec as P
 
+MESH = pl.DeviceIdType.MESH
+MIB = 1024 * 1024
+GROUPS = 32
+PIECES = (3, 2, 2, 4, 2, 96, 768)
+
+class Pos: pass
+def position(F, r):
+    p = Pos()
+    L = lax.axis_index("dp")*F + lax.axis_index("fsdp")
+    g = lax.div(L, r); p.rho = lax.rem(L, r); p.F=F; p.r=r
+    p.g=g
+    p.c = lax.rem(g,2); p.z = lax.rem(lax.div(g,2),4); p.x = lax.rem(lax.div(g,8),2); p.y = lax.div(g,16)
+    p.l = p.y + p.c*(p.x-p.y); p.f = p.x + p.c*(p.y-p.x)
+    def dev(y,x,z,c):
+        L2 = (((y*2+x)*4+z)*2+c)*r + p.rho
+        return (lax.div(L2,F), lax.rem(L2,F))
+    c,x,y,z = p.c,p.x,p.y,p.z
+    p.dev=dev
+    p.sib = dev(y,x,z,1-c)
+    p.fn = dev(y + c*(1-2*y), x + (1-c)*(1-2*x), z, c)
+    p.ln = dev(y + (1-c)*(1-2*y), x + c*(1-2*x), z, c)
+    p.up = dev(y,x,jnp.minimum(z+1,3),c)
+    p.dn = dev(y,x,jnp.maximum(z-1,0),c)
+    return p
+
+def barrier(p):
+    bar = pltpu.get_barrier_semaphore()
+    def body(i, _):
+        q = lax.rem(lax.div(p.g,2) + i, 16)
+        L2 = (q*2+p.c)*p.r + p.rho
+        pl.semaphore_signal(bar, inc=1, device_id=(lax.div(L2,p.F), lax.rem(L2,p.F)), device_id_type=MESH)
+        return 0
+    lax.fori_loop(1, 16, body, 0)
+    pl.semaphore_signal(bar, inc=1, device_id=p.sib, device_id_type=MESH)
+    pl.semaphore_wait(bar, 16)
+
+class Gather:
+    def __init__(s, p, W, m, sems):
+        s.p, s.W, s.m = p, W, m
+        s.ss, s.rs = sems
+    def cp(s, idx, ks, kr, dev):
+        ref = s.W.at[(s.m,)+idx]
+        return pltpu.make_async_remote_copy(src_ref=ref, dst_ref=ref, send_sem=s.ss.at[s.m, ks], recv_sem=s.rs.at[s.m, kr], device_id=dev, device_id_type=MESH)
+    def f(s):
+        p=s.p; return s.cp((p.c,p.l,p.z,p.f), 0, 0, p.fn)
+    def f_in(s):
+        p=s.p; return s.cp((p.c,p.l,p.z,1-p.f), 0, 0, p.fn)
+    def fb(s, b):
+        return s.p.f + b*(1-2*s.p.f)
+    def up(s, zz, b): f=s.fb(b); return s.cp((s.p.c,s.p.l,zz,f), 1+2*zz+b, 1+2*zz+b, s.p.up)
+    def dn(s, zz, b): f=s.fb(b); return s.cp((s.p.c,s.p.l,zz,f), 9+2*zz+b, 1+2*zz+b, s.p.dn)
+    def ll(s, zz): return s.cp((s.p.c,s.p.l,zz), 17+zz, 9+zz, s.p.ln)
+    def l_in(s, zz): return s.cp((s.p.c,1-s.p.l,zz), 17+zz, 9+zz, s.p.ln)
+    def d(s, l, zz): return s.cp((s.p.c,l,zz), 21+4*l+zz, 13+4*l+zz, s.p.sib)
+    def d_in(s, l, zz): return s.cp((1-s.p.c,l,zz), 21+4*l+zz, 13+4*l+zz, s.p.sib)
+    def own(s, b):
+        p=s.p
+        if b: s.f_in().wait_recv()
+        else: s.f().start()
+        @pl.when(p.z<3)
+        def _(): s.up(p.z,b).start()
+        @pl.when(p.z>0)
+        def _(): s.dn(p.z,b).start()
+        if b:
+            s.ll(p.z).start()
+            s.d(p.l, p.z).start()
+    def stepz(s, h, b):
+        p=s.p
+        @pl.when(p.z-h>=0)
+        def _():
+            zz=p.z-h
+            s.up(zz,b).wait_recv()
+            @pl.when(p.z<3)
+            def _(): s.up(zz,b).start()
+            if b: s.ll(zz).start(); s.d(p.l,zz).start()
+        @pl.when(p.z+h<=3)
+        def _():
+            zz=p.z+h
+            s.dn(zz,b).wait_recv()
+            @pl.when(p.z>0)
+            def _(): s.dn(zz,b).start()
+            if b: s.ll(zz).start(); s.d(p.l,zz).start()
+    def stepl(s, h):
+        p=s.p
+        def one(zz):
+            s.l_in(zz).wait_recv(); s.d(1-p.l,zz).start()
+        if h==0: one(p.z)
+        else:
+            @pl.when(p.z-h>=0)
+            def _(): one(p.z-h)
+            @pl.when(p.z+h<=3)
+            def _(): one(p.z+h)
+    def finish(s):
+        for zz in range(4):
+            for l in range(2): s.d_in(l,zz).wait_recv()
+    def drain(s):
+        p=s.p
+        s.f().wait_send()
+        for zz in range(4):
+            @pl.when((p.z<3) & (zz<=p.z))
+            def _(): s.up(zz,0).wait_send(); s.up(zz,1).wait_send()
+            @pl.when((p.z>0) & (zz>=p.z))
+            def _(): s.dn(zz,0).wait_send(); s.dn(zz,1).wait_send()
+            s.ll(zz).wait_send()
+            for l in range(2): s.d(l,zz).wait_send()
+
+class Scatter:
+    def __init__(s, p, G, m, R, X, sems):
+        s.p, s.G, s.m, s.R, s.X = p, G, m, R, X
+        s.ss, s.rs = sems
+    def cp(s, src, dst, ks, kr, dev):
+        return pltpu.make_async_remote_copy(src_ref=src, dst_ref=dst, send_sem=s.ss.at[s.m, ks], recv_sem=s.rs.at[s.m, kr], device_id=dev, device_id_type=MESH)
+    def gq(s, c, l): return s.G.at[s.m, c, l]
+    def rc(s, l): return s.R.at[l]
+    def ra(s, zz): return s.R.at[2, zz]
+    def c_cp(s, l): return s.cp(s.gq(1-s.p.c, l), s.rc(l), 1+l, 1+l, s.p.sib)
+    def a_cp(s, zz): return s.cp(s.G.at[s.m, s.p.c, 1-s.p.l, zz], s.ra(zz), 3+zz, 3+zz, s.p.ln)
+    def fb(s, b): return 1-s.p.f if b==0 else s.p.f
+    def zsrc(s, zz, b): return s.G.at[s.m, s.p.c, s.p.l, zz, s.fb(b)]
+    def up_far(s, zz, b): return s.cp(s.zsrc(zz,b), s.R.at[3, zz, b], 7+2*zz+b, 7+2*zz+b, s.p.up)
+    def up_end(s, zz, b): return s.cp(s.zsrc(zz,b), s.X.at[b], 7+2*zz+b, 15+b, s.p.up)
+    def down(s, zz, b): return s.cp(s.zsrc(zz,b), s.R.at[3, zz, b], 15+2*zz+b, 7+2*zz+b, s.p.dn)
+    def f_cp(s): return s.cp(s.zsrc(s.p.z, 0), s.X.at[2], 0, 0, s.p.fn)
+    def c_send(s, l): s.c_cp(l).start()
+    def c_add(s, l):
+        s.c_cp(l).wait_recv()
+        def body(zz, _):
+            for ff in range(2):
+                g = s.G.at[s.m, s.p.c, l, zz, ff]
+                g[...] = (g[...].astype(jnp.float32) + s.R[l, zz, ff].astype(jnp.float32)).astype(jnp.bfloat16)
+            return 0
+        lax.fori_loop(0, 4, body, 0)
+    def add(s, zz, b, ref):
+        g = s.zsrc(zz, b)
+        g[...] = (g[...].astype(jnp.float32) + ref[...].astype(jnp.float32)).astype(jnp.bfloat16)
+    def by_dist(s, h, fn):
+        p=s.p
+        if h==0: fn(p.z); return
+        @pl.when(p.z+h<=3)
+        def _(): fn(p.z+h)
+        @pl.when(p.z-h>=0)
+        def _(): fn(p.z-h)
+    def a_send(s):
+        for h in (3,2,1,0): s.by_dist(h, lambda zz: s.a_cp(zz).start())
+    def a_add(s, h):
+        def one(zz):
+            s.a_cp(zz).wait_recv()
+            for b in (0,1):
+                g = s.zsrc(zz,b)
+                g[...] = (g[...].astype(jnp.float32) + s.R[2, zz, s.fb(b)].astype(jnp.float32)).astype(jnp.bfloat16)
+        s.by_dist(h, one)
+    def z_step(s, h, b):
+        p=s.p
+        if h>0:
+            @pl.when(p.z+h<=3)
+            def _():
+                zz=p.z+h
+                @pl.when(p.z>0)
+                def _():
+                    s.up_far(zz,b).wait_recv(); s.add(zz,b,s.R.at[3,zz,b])
+                if h==1: s.up_end(zz,b).start()
+                else: s.up_far(zz,b).start()
+            @pl.when(p.z-h>=0)
+            def _():
+                zz=p.z-h
+                @pl.when(p.z<3)
+                def _():
+                    s.down(zz,b).wait_recv(); s.add(zz,b,s.R.at[3,zz,b])
+                s.down(zz,b).start()
+        else:
+            @pl.when(p.z>0)
+            def _():
+                s.up_end(p.z,b).wait_recv(); s.add(p.z,b,s.X.at[b])
+            @pl.when(p.z<3)
+            def _():
+                s.down(p.z,b).wait_recv(); s.add(p.z,b,s.R.at[3,p.z,b])
+            if b==0: s.f_cp().start()
+    def final(s):
+        s.f_cp().wait_recv()
+        return s.zsrc(s.p.z,1)[...].astype(jnp.float32) + s.X[2].astype(jnp.float32)
+    def drain(s):
+        p=s.p
+        for l in range(2): s.c_cp(l).wait_send()
+        for zz in range(4):
+            s.a_cp(zz).wait_send()
+            @pl.when(zz>p.z)
+            def _():
+                for b in (0,1): s.up_far(zz,b).wait_send()
+            @pl.when(zz<p.z)
+            def _():
+                for b in (0,1): s.down(zz,b).wait_send()
+        s.f_cp().wait_send()
+
+
+def gather_kernel(F, r, own, w_out, W, ss, rs):
+    p = position(F, r)
+    for m in range(3):
+        W[m, p.c, p.l, p.z, p.f] = own[m]
+    barrier(p)
+    gs = [Gather(p, W, m, (ss, rs)) for m in range(3)]
+    gs[0].own(0); gs[0].own(1)
+    for m in range(3):
+        g=gs[m]
+        g.stepz(1,0); g.stepz(1,1); g.stepl(0)
+        g.stepz(2,0); g.stepz(2,1)
+        if m<2: gs[m+1].own(0)
+        g.stepl(1)
+        if m<2: gs[m+1].own(1)
+        g.stepz(3,0); g.stepz(3,1); g.stepl(2)
+        g.stepl(3)
+    for g in gs: g.finish()
+    w_out[...] = W[...]
+    for g in gs: g.drain()
+
+
+def scatter_kernel(F, r, g_ref, o_ref, G, R, X, ss, rs):
+    p = position(F, r)
+    G[...] = g_ref[...]
+    barrier(p)
+    sc=[Scatter(p, G, m, R.at[m], X.at[m], (ss,rs)) for m in range(3)]
+    for m in range(3): sc[m].c_send(1-p.f)
+    for m in range(3): sc[m].c_send(p.f)
+    for m in range(3):
+        s=sc[m]
+        s.c_add(1-p.l); s.a_send(); s.c_add(p.l)
+    for m in range(3):
+        s=sc[m]
+        for h in (3,2,1,0):
+            s.a_add(h)
+            for b in (0,1): s.z_step(h,b)
+        o_ref[m] = s.final()
+    for s in sc: s.drain()
+
+
+def swap(block, step):
+    return lambda size: lax.ppermute(block, "fsdp", [(i, i ^ step) for i in range(size)])
+
+
+def pregather(block, F, r):
+    step = 1
+    while step < r:
+        high = (lax.axis_index("fsdp") // step) % 2 == 1
+        other = swap(block, step)(F)
+        block = jnp.concatenate([jnp.where(high, other, block), jnp.where(high, block, other)], 0)
+        step *= 2
+    return block
+
+
+def postscatter(block, F, r):
+    step = r // 2
+    while step:
+        high = (lax.axis_index("fsdp") // step) % 2 == 1
+        half = block.shape[0] // 2
+        keep = jnp.where(high, block[half:], block[:half])
+        send = jnp.where(high, block[:half], block[half:])
+        block = keep + swap(send, step)(F)
+        step //= 2
+    return block
+
+
+def to_natural(pieces):
+    zero = pieces[:, 0].transpose(0, 1, 3, 2, 4, 5)
+    one = pieces[:, 1].transpose(0, 3, 1, 2, 4, 5)
+    return jnp.stack([zero, one], 4).reshape(3, 32, 96, 768)
+
+
+def to_pieces(natural):
+    both = natural.reshape(3, 2, 2, 4, 2, 96, 768)
+    zero = both[:, :, :, :, 0].transpose(0, 1, 3, 2, 4, 5)
+    one = both[:, :, :, :, 1].transpose(0, 2, 3, 1, 4, 5)
+    return jnp.stack([zero, one], 1)
+
 HEADS = 12
-MICRO = 3
-
 
 norm_eps = 1e-06
 
@@ -187,7 +460,37 @@
     return (grad_input, grad_list)
 
 
+def gather_weights(F, r, own):
+    return pl.pallas_call(
+        functools.partial(gather_kernel, F, r),
+        out_shape=jax.ShapeDtypeStruct(PIECES, jnp.bfloat16),
+        in_specs=[pl.BlockSpec(memory_space=pltpu.VMEM)],
+        out_specs=pl.BlockSpec(memory_space=pltpu.VMEM),
+        scratch_shapes=[pltpu.VMEM(PIECES, jnp.bfloat16), pltpu.SemaphoreType.DMA((3, 32)), pltpu.SemaphoreType.DMA((3, 32))],
+        compiler_params=pltpu.CompilerParams(collective_id=0, has_side_effects=True, vmem_limit_bytes=60 * MIB),
+    )(own)
+
+
+def scatter_grads(F, r, pieces):
+    return pl.pallas_call(
+        functools.partial(scatter_kernel, F, r),
+        out_shape=jax.ShapeDtypeStruct((3, 96, 768), jnp.float32),
+        in_specs=[pl.BlockSpec(memory_space=pltpu.VMEM)],
+        out_specs=pl.BlockSpec(memory_space=pltpu.VMEM),
+        scratch_shapes=[
+            pltpu.VMEM(PIECES, jnp.bfloat16),
+            pltpu.VMEM((3, 4, 4, 2, 96, 768), jnp.bfloat16),
+            pltpu.VMEM((3, 3, 96, 768), jnp.bfloat16),
+            pltpu.SemaphoreType.DMA((3, 32)),
+            pltpu.SemaphoreType.DMA((3, 32)),
+        ],
+        compiler_params=pltpu.CompilerParams(collective_id=1, has_side_effects=True, vmem_limit_bytes=62 * MIB),
+    )(pieces)
+
+
 def per_device(
+    F,
+    r,
     images,
     tissue,
     pair_index,
@@ -208,7 +511,14 @@
     cotangent,
 ):
     local_images, slot_count, model_width = images.shape
-    per_micro = local_images // MICRO
+    per_micro = local_images
+    MICRO = 1
+    own = jnp.stack([jnp.concatenate([pregather(w_qkv.T, F, r), pregather(w_out.T, F, r)], 0), pregather(w_fc1.T, F, r), pregather(w_fc2, F, r)], 0)
+    full = to_natural(gather_weights(F, r, own))
+    w_qkv_t = full[0, :, :72].reshape(-1, model_width)
+    w_out_t = full[0, :, 72:].reshape(-1, model_width)
+    w_fc1_t = full[1].reshape(-1, model_width)
+    w_fc2_f = full[2].reshape(-1, model_width)
     tissue_float = tissue.astype(jnp.float32)
     saved_all = []
     pooled_parts = []
@@ -217,15 +527,15 @@
         params_full = (
             lax.all_gather(ln1_gain, ("dp", "fsdp"), axis=0, tiled=True),
             lax.all_gather(ln1_bias, ("dp", "fsdp"), axis=0, tiled=True),
-            lax.all_gather(w_qkv, ("dp", "fsdp"), axis=1, tiled=True),
+            w_qkv_t.T,
             lax.all_gather(bias_qv, ("dp", "fsdp"), axis=0, tiled=True),
-            lax.all_gather(w_out, ("dp", "fsdp"), axis=1, tiled=True),
+            w_out_t.T,
             lax.all_gather(bias_out, ("dp", "fsdp"), axis=0, tiled=True),
             lax.all_gather(ln2_gain, ("dp", "fsdp"), axis=0, tiled=True),
             lax.all_gather(ln2_bias, ("dp", "fsdp"), axis=0, tiled=True),
-            lax.all_gather(w_fc1, ("dp", "fsdp"), axis=1, tiled=True),
+            w_fc1_t.T,
             lax.all_gather(bias_fc1, ("dp", "fsdp"), axis=0, tiled=True),
-            lax.all_gather(w_fc2, ("dp", "fsdp"), axis=0, tiled=True),
+            w_fc2_f,
             lax.all_gather(bias_fc2, ("dp", "fsdp"), axis=0, tiled=True),
         )
         first_image = micro_step * per_micro
@@ -301,15 +611,15 @@
         params_full = (
             lax.all_gather(ln1_gain, ("dp", "fsdp"), axis=0, tiled=True),
             lax.all_gather(ln1_bias, ("dp", "fsdp"), axis=0, tiled=True),
-            lax.all_gather(w_qkv, ("dp", "fsdp"), axis=1, tiled=True),
+            w_qkv_t.T,
             lax.all_gather(bias_qv, ("dp", "fsdp"), axis=0, tiled=True),
-            lax.all_gather(w_out, ("dp", "fsdp"), axis=1, tiled=True),
+            w_out_t.T,
             lax.all_gather(bias_out, ("dp", "fsdp"), axis=0, tiled=True),
             lax.all_gather(ln2_gain, ("dp", "fsdp"), axis=0, tiled=True),
             lax.all_gather(ln2_bias, ("dp", "fsdp"), axis=0, tiled=True),
-            lax.all_gather(w_fc1, ("dp", "fsdp"), axis=1, tiled=True),
+            w_fc1_t.T,
             lax.all_gather(bias_fc1, ("dp", "fsdp"), axis=0, tiled=True),
-            lax.all_gather(w_fc2, ("dp", "fsdp"), axis=0, tiled=True),
+            w_fc2_f,
             lax.all_gather(bias_fc2, ("dp", "fsdp"), axis=0, tiled=True),
         )
         first_image = micro_step * per_micro
@@ -335,18 +645,20 @@
             grad_totals = grad_list
         else:
             grad_totals = jax.tree.map(jnp.add, grad_totals, grad_list)
+    natural = jnp.stack([jnp.concatenate([grad_totals[2].T.reshape(32, 72, -1), grad_totals[4].T.reshape(32, 24, -1)], 1), grad_totals[8].T.reshape(32, 96, -1), grad_totals[10].reshape(32, 96, -1)], 0)
+    mine = scatter_grads(F, r, to_pieces(natural.astype(jnp.bfloat16)))
     shares = (
         lax.psum_scatter(grad_totals[0], ("dp", "fsdp"), scatter_dimension=0, tiled=True),
         lax.psum_scatter(grad_totals[1], ("dp", "fsdp"), scatter_dimension=0, tiled=True),
-        lax.psum_scatter(grad_totals[2], ("dp", "fsdp"), scatter_dimension=1, tiled=True),
+        postscatter(mine[0, :72], F, r).T,
         lax.psum_scatter(grad_totals[3], ("dp", "fsdp"), scatter_dimension=0, tiled=True),
-        lax.psum_scatter(grad_totals[4], ("dp", "fsdp"), scatter_dimension=1, tiled=True),
+        postscatter(mine[0, 72:], F, r).T,
         lax.psum_scatter(grad_totals[5], ("dp", "fsdp"), scatter_dimension=0, tiled=True),
         lax.psum_scatter(grad_totals[6], ("dp", "fsdp"), scatter_dimension=0, tiled=True),
         lax.psum_scatter(grad_totals[7], ("dp", "fsdp"), scatter_dimension=0, tiled=True),
-        lax.psum_scatter(grad_totals[8], ("dp", "fsdp"), scatter_dimension=1, tiled=True),
+        postscatter(mine[1], F, r).T,
         lax.psum_scatter(grad_totals[9], ("dp", "fsdp"), scatter_dimension=0, tiled=True),
-        lax.psum_scatter(grad_totals[10], ("dp", "fsdp"), scatter_dimension=0, tiled=True),
+        postscatter(mine[2], F, r),
         lax.psum_scatter(grad_totals[11], ("dp", "fsdp"), scatter_dimension=0, tiled=True),
     )
     input_grad = jnp.concatenate(input_parts, 0)
@@ -371,6 +683,8 @@
 
 
 def solution(mesh):
+    F = mesh.shape["fsdp"]
+    r = mesh.shape["dp"] * F // GROUPS
     in_specs = (
         P(("dp", "fsdp"), None, None),
         P(("dp", "fsdp"), None),
@@ -410,5 +724,5 @@
         P(("dp", "fsdp")),
     )
     return jax.shard_map(
-        per_device, mesh=mesh, in_specs=in_specs, out_specs=out_specs, check_vma=False
-    )
+        functools.partial(per_device, F, r), mesh=mesh, in_specs=in_specs, out_specs=out_specs, check_vma=False
+    )

time: 961 us -> 698 us (0.73)
  waiting for transfers between devices: 484 us -> 0 us
  Pallas kernels: 0 us -> 158 us
  local copies, waits for them, and re-layouts: 36.5 us -> 124 us
  matrix products: 136 us -> 89.7 us
  other arithmetic: 31.5 us -> 68.8 us
  between operations: 20.1 us -> 5.75 us
    reduce_scatter x4 -> x0, waiting for transfers between devices: 368 us -> none  [the longest x1 142 us: per_device(): lax.psum_scatter(grad_totals[10], ('dp', 'fsdp'), scatter_dimension=0, ti...]
    pallas_call x0 -> x2, Pallas kernels: none -> 158 us  [the longest x1 82 us: scatter_grads(): pl.pallas_call(functools.partial(scatter_kernel, F, r), out_shape=jax.Sha...]
    all_gather x4 -> x0, waiting for transfers between devices: 114 us -> none  [the longest x1 55.1 us: per_device(): lax.all_gather(w_fc2, ('dp', 'fsdp'), axis=0, tiled=True)]
    slice x2 -> x6, local copies, waits for them, and re-layouts: 0.04 us -> 24.4 us  [the longest x1 8.34 us: to_natural(): zero = pieces[:, 0].transpose(0, 1, 3, 2, 4, 5)]
    reshape x0 -> x6, local copies, waits for them, and re-layouts: none -> 19.9 us  [the longest x2 8.38 us: backward_block(): grad_attended = grad_attended.reshape(values.shape)]
    convert_element_type x0 -> x2, other arithmetic: none -> 19.8 us  [the longest x1 18.2 us: forward_block(): activated = exact_gelu(pre_act).astype(jnp.bfloat16)]
    convert_element_type x6 -> x10, local copies, waits for them, and re-layouts: 9.16 us -> 28.7 us  [the longest x2 15.5 us: backward_block(): grad_joined = jnp.stack([grad_queries, grad_keys, grad_values], 2).reshap...]
    another operation x0 -> x6, other arithmetic: none -> 19.4 us  [the longest x1 5.67 us: per_device(): jnp.stack([jnp.concatenate([grad_totals[2].T.reshape(32, 72, -1), grad_to...]
  transfers between devices with their start and end apart: 8 -> 0, of which waited for: 6 -> 0; matrix products, arithmetic and copies ran while one was open for 10% -> 0% of each run, Pallas kernels for 0% -> 0%
where the time goes in v1:
time: 698 us; the launch traced here: 691 us
  blocking collectives  245 us (35%)
  Pallas kernels  158 us (23%)
  local copies, waits for them, and re-layouts  124 us (18%)
  matrix products  89.7 us (13%)
  other arithmetic  68.8 us (10%)
    unnamed x4, blocking collectives  163 us
    pallas_call x1, Pallas kernels, scatter_grads(): pl.pallas_call(functools.partial(scatter_kernel, F, r), out_shape=jax.Sha...  82 us
    pallas_call x1, Pallas kernels, gather_weights(): pl.pallas_call(functools.partial(gather_kernel, F, r), out_shape=jax.Shap...  76.5 us
    all_gather x1, blocking collectives, per_device(): lax.all_gather(text_unit, ('dp', 'fsdp'), axis=0, tiled=True)  42 us
    all_gather x1, blocking collectives, per_device(): lax.all_gather(image_unit, ('dp', 'fsdp'), axis=0, tiled=True)  40.1 us
    unnamed x155, local copies, waits for them, and re-layouts  36.5 us
    dot_general x1, matrix products, forward_block(): jnp.dot(second, w_fc1, preferred_element_type=jnp.float32)  20 us
    convert_element_type x1, other arithmetic, forward_block(): activated = exact_gelu(pre_act).astype(jnp.bfloat16)  18.2 us

profile of v1, /device:TPU:0, one launch (start us, length us, event | category | flops | bytes accessed | tf_op | source)
XLA Modules:
  0.0 691.5 jit_solution(577190648865095034)
XLA Ops:
  4.9 42.0 %all-reduce.11 = s32[96]{0:T(128)} all-reduce(s32[96]{0:T(128)S(1)} %dynamic-update-slice.11), channel_id=1, replica_groups=mesh['dp'=4,'fsdp'=8] {'dp','fsdp'}, use_global_device_ids=true, to_apply=%add.11 | all-reduce | flops 96 | bytes 768
  53.4 1.4 convert_reduce_fusion.4
  55.5 1.6 multiply_reduce_fusion.1
  60.3 40.7 %all-reduce.21 = (bf16[768]{0:T(1024)(128)(2,1)S(1)}, bf16[768]{0:T(1024)(128)(2,1)S(1)}, bf16[1536]{0:T(1024)(128)(2,1)S(1)}, bf16[768]{0:T(1024)(128)(2,1)S(1)...) all-reduce(bf16[768]{0:T(1024)(128)(2,1)S(1)} %dynamic-update-slice, ...), channel_id=1, replica_groups=mesh['dp'=4,'fsdp'=8] {'dp','fsdp'}, use_global_device_ids=true, to_apply=%add.1 | all-reduce | flops 9216 | bytes 36864
  102.0 42.0 %all-gather = bf16[32,3,768]{2,1,0:T(4,128)(2,1)S(1)} all-gather(bf16[1,3,768]{2,1,0:T(4,128)(2,1)S(1)} %fusion.83), channel_id=1, replica_groups=mesh['dp'=4,'fsdp'=8] {'dp','fsdp'}, dimensions={0}, use_global_device_ids=true | all-gather | bytes 152064 | tf_op jit(solution)/shard_map/all_gather | solution.py:561
  144.8 1.8 pad_maximum_fusion.4.own
  146.6 1.6 add_convert_fusion.2
  150.3 1.4 reshape.315
  151.7 76.5 %shard_map.297 = bf16[3,2,2,4,2,96,768]{6,5,4,3,2,1,0:T(8,128)(2,1)} custom-call(bf16[3,96,768]{2,1,0:T(8,128)(2,1)} %pad_maximum_fusion.4.own), custom_call_target="tpu_custom_call" | custom-call | tf_op jit(solution)/shard_map/pallas_call | solution.py:464
  228.2 8.3 %fusion.92 = (bf16[3,1,2,4,2,96,768]{6,5,4,3,2,1,0:T(8,128)(2,1)}, bf16[3,2,2,4,1,96,768]{6,5,1,3,2,0,4:T(8,128)(2,1)S(1)}) fusion(bf16[3,2,2,4,2,96,768]{6,5,4,3,2,1,0:T(8,128)(2,1)} %shard_map.297), kind=kLoop, calls=%fused_computation.192 | loop fusion | bytes 28311552 | tf_op jit(solution)/shard_map/slice | solution.py:270
  236.5 3.6 copy.124
  240.2 4.0 fusion.25
  244.2 1.4 pad_maximum_fusion
  245.6 2.7 copy.73
  248.3 2.6 copy.80
  252.2 1.7 copy-done.18
  253.9 2.3 add_convert_fusion.1
  256.3 7.0 %reshape.349 = bf16[3,196,3,12,64]{4,3,2,1,0:T(8,128)(2,1)} reshape(bf16[588,2304]{1,0:T(8,128)(2,1)S(1)} %add_convert_fusion.1) | data formatting | bytes 5419008 | tf_op jit(solution)/shard_map/reshape | solution.py:303
  263.3 6.8 fusion.93
  270.1 2.9 copy.110
  272.9 3.3 copy.111
  276.3 3.8 copy.112
  280.1 5.4 copy.81
  285.4 1.9 fusion.36
  287.4 1.9 fusion.23
  289.3 2.1 fusion.43
  292.5 2.4 convert_element_type.171
  295.0 2.8 fusion.97
  298.1 20.0 %fusion = (f32[588,3072]{1,0:T(8,128)S(1)}, f32[588,3072]{1,0:T(8,128)S(1)}) fusion(f32[3072]{0:T(1024)S(1)} %convert_element_type.176, bf16[3072,768]{1,0:T(8,128)(2,1)} %bitcast.204, f32[588,768]{1,0:T(8,128)S(1)} %get-tuple-element.83, f32[768]{0:T(1024)S(1)} %convert_element_type.174, f32[768]{0:T(1024)S(1)} %convert_element_type.173, ...), kind=kOutput, calls=%fused_computation.15 | convolution fusion | flops 2890589184 | bytes 20998752 | tf_op jit(solution)/shard_map/dot_general | solution.py:356
  318.2 3.0 copy-done.10
  321.1 2.1 copy-done.52
  323.3 4.3 add_multiply_fusion.2
  327.6 1.6 reshape.310
  332.9 40.1 %all-gather.1 = bf16[32,3,768]{2,1,0:T(4,128)(2,1)S(1)} all-gather(bf16[1,3,768]{2,1,0:T(4,128)(2,1)S(1)} %fusion.84), channel_id=1, replica_groups=mesh['dp'=4,'fsdp'=8] {'dp','fsdp'}, dimensions={0}, use_global_device_ids=true | all-gather | bytes 152064 | tf_op jit(solution)/shard_map/all_gather | solution.py:562
  374.3 37.0 %all-reduce.8 = f32[96]{0:T(128)S(1)} all-reduce(f32[96]{0:T(128)S(1)} %get-tuple-element.56), channel_id=1, replica_groups=mesh['dp'=4,'fsdp'=8] {'dp','fsdp'}, use_global_device_ids=true, to_apply=%add.8 | all-reduce | flops 96 | bytes 768
  412.3 2.1 convert_reduce_fusion.2
  414.8 10.2 %convert_reduce_fusion = (f32[3072]{0:T(1024)}, bf16[588,3072]{1,0:T(8,128)(2,1)S(1)}) fusion(f32[588,3072]{1,0:T(8,128)} %copy-done.52, f32[588,3072]{1,0:T(8,128)} %copy-done.10, f32[3072]{0:T(1024)S(1)} %convert_element_type.176, bf16[588,768]{1,0:T(8,128)(2,1)S(1)} %convert_element_type.187, bf16[3072,768]{1,0:T(8,128)(2,1)} %bitcast.208), kind=kOutput, calls=%fused_computation.24 | convolution fusion | flops 2805236736 | bytes 23709696 | tf_op jit(solution)/shard_map/nd,fd->nf/dot_general | solution.py:391
  424.9 18.2 %fusion.3 = bf16[3072,588]{0,1:T(8,128)(2,1)} fusion(f32[588,3072]{1,0:T(8,128)} %copy-done.10, f32[3072]{0:T(1024)S(1)} %convert_element_type.176), kind=kLoop, calls=%fused_computation.18 | loop fusion | flops 119218176 | bytes 10850304 | tf_op jit(solution)/shard_map/convert_element_type | solution.py:359
  443.1 3.9 multiply_reduce_fusion.2
  447.0 1.9 fusion.90
  448.9 6.0 convolution_convert_fusion
  454.9 6.0 copy.91
  461.0 8.0 %convert_bitcast_fusion = bf16[1,2,2,4,2,96,768]{6,5,1,3,2,0,4:T(8,128)(2,1)} fusion(bf16[2,2,4,2,96,588]{5,4,3,2,1,0:T(8,128)(2,1)} %bitcast.212, bf16[588,768,1,1,1,1]{1,0,2,3,4,5:T(8,128)(2,1)S(1)} %reshape.346), kind=kOutput, calls=%fused_computation.67 | convolution fusion | flops 2776891392 | bytes 9234432 | tf_op jit(solution)/shard_map/nf,nd->fd/dot_general | solution.py:387
  468.9 1.5 reshape.311
  470.4 3.0 convert_reduce_fusion.3
  473.5 3.1 convolution_convert_fusion.3
  477.9 3.7 convolution_convert_fusion.2
  481.6 4.0 reshape.350
  485.6 4.3 copy.83
  490.0 5.3 fusion.39
  495.4 3.0 multiply_reduce_fusion
  498.4 2.9 multiply_convert_fusion
  508.6 5.6 copy.88
  514.1 10.0 %convert_element_type.194 = bf16[588,2304]{0,1:T(8,128)(2,1)} reshape(bf16[3,196,3,12,64]{1,0,4,3,2:T(4,128)(2,1)} %copy.88) | data formatting | bytes 5419008 | tf_op jit(solution)/shard_map/convert_element_type | solution.py:435
  524.2 5.8 multiply_reduce_fusion.3
  532.0 3.2 convolution_convert_fusion.1
  535.8 5.7 pad_maximum_fusion.1
  542.8 5.6 pad_maximum_fusion.2.g_ref
  548.5 82.0 %shard_map.298 = f32[3,96,768]{2,1,0:T(8,128)} custom-call(bf16[3,2,2,4,2,96,768]{6,5,4,3,2,1,0:T(8,128)(2,1)} %pad_maximum_fusion.2.g_ref), custom_call_target="tpu_custom_call" | custom-call | tf_op jit(solution)/shard_map/pallas_call | solution.py:475
  630.5 43.0 %all-reduce.20 = (f32[96]{0:T(128)S(1)}, f32[96]{0:T(128)S(1)}, f32[768]{0:T(1024)S(1)}, f32[768]{0:T(1024)S(1)}, f32[1536]{0:T(1024)S(1)}, /*index=5*/f32[768]{...) all-reduce(f32[96]{0:T(128)S(1)} %copy-done.49, ...), channel_id=1, replica_groups=mesh['dp'=4,'fsdp'=8] {'dp','fsdp'}, use_global_device_ids=true, to_apply=%add.9 | all-reduce | flops 9408 | bytes 75264
  683.7 1.4 reshape.313
  685.0 1.5 slice_bitcast_fusion.6
  686.6 1.6 slice_bitcast_fusion.5
  688.2 1.9 slice_bitcast_fusion.3
  (220 shorter events, 47.4 us)
Async XLA Ops:
  0.6 149.7 %copy-start.5 = (bf16[3,196,768]{2,1,0:T(8,128)(2,1)S(1)}, bf16[3,196,768]{2,1,0:T(8,128)(2,1)}, u32[]{:S(2)}) copy-start(bf16[3,196,768]{2,1,0:T(8,128)(2,1)} %param.18) | copy-start | bytes 2709508
  4.0 47.8 %copy-start.51 = (f32[3]{0:T(128)}, f32[3]{0:T(128)S(1)}, u32[]{:S(2)}) copy-start(f32[3]{0:T(128)S(1)} %fusion.57) | copy-start | bytes 40
  4.1 54.6 %copy-start.43 = (f32[3]{0:T(128)}, f32[3]{0:T(128)S(1)}, u32[]{:S(2)}) copy-start(f32[3]{0:T(128)S(1)} %add_rsqrt_fusion) | copy-start | bytes 40
  53.3 4.6 copy-start.32
  58.0 43.0 %copy-start.30 = (f32[588]{0:T(1024)}, f32[588]{0:T(1024)S(1)}, u32[]{:S(2)}) copy-start(f32[588]{0:T(1024)S(1)} %add.201) | copy-start | bytes 7060
  101.0 127.2 %copy-start.28 = (f32[768]{0:T(1024)}, f32[768]{0:T(1024)S(1)}, u32[]{:S(2)}) copy-start(f32[768]{0:T(1024)S(1)} %convert_element_type.161) | copy-start | bytes 9220
  245.6 2.7 copy-start.1
  250.9 3.1 copy-start.23
  252.2 1.7 copy-start.18
  276.3 11.1 %copy-start.6 = (bf16[3,196,1,12,64]{1,4,3,0,2:T(8,128)(2,1)}, bf16[3,196,1,12,64]{1,4,3,0,2:T(8,128)(2,1)S(1)}, u32[]{:S(2)}) copy-start(bf16[3,196,1,12,64]{1,4,3,0,2:T(8,128)(2,1)S(1)} %copy.111) | copy-start | bytes 2709508
  280.1 7.3 %copy-start.8 = (bf16[3,196,1,12,64]{1,4,3,0,2:T(8,128)(2,1)}, bf16[3,196,1,12,64]{1,4,3,0,2:T(8,128)(2,1)S(1)}, u32[]{:S(2)}) copy-start(bf16[3,196,1,12,64]{1,4,3,0,2:T(8,128)(2,1)S(1)} %copy.112) | copy-start | bytes 2709508
  285.4 3.9 copy-start.15
  287.4 4.1 copy-start
  289.3 5.6 copy-start.13
  295.0 28.3 %slice-start.4 = ((s8[4718592]{0:T(1024)(128)(4,1)}), s8[4194304]{0:T(1024)(128)(4,1)S(1)}, s32[]{:S(2)}) async-start(s8[4718592]{0:T(1024)(128)(4,1)} %bitcast.209), calls=%async_computation.4 | async-start | bytes 8388608
  297.7 20.4 %copy-start.11 = (f32[588,768]{1,0:T(8,128)}, f32[588,768]{1,0:T(8,128)S(1)}, u32[]{:S(2)}) copy-start(f32[588,768]{1,0:T(8,128)S(1)} %get-tuple-element.83) | copy-start | bytes 5419012
  298.1 25.1 %slice-start.5 = ((s8[4718592]{0:T(1024)(128)(4,1)}), s8[524288]{0:T(1024)(128)(4,1)S(1)}, s32[]{:S(2)}) async-start(s8[4718592]{0:T(1024)(128)(4,1)} %bitcast.209), calls=%async_computation.5 | async-start | bytes 1048576
  318.1 3.0 copy-start.10
  318.2 5.1 copy-start.52
  323.2 7.0 %copy-start.40 = (f32[3]{0:T(128)S(1)}, f32[3]{0:T(128)}, u32[]{:S(2)}) copy-start(f32[3]{0:T(128)} %convert_reduce_fusion.5) | copy-start | bytes 40
  323.2 7.2 %copy-start.26 = (bf16[96,768]{1,0:T(8,128)(2,1)S(1)}, bf16[96,768]{1,0:T(8,128)(2,1)}, u32[]{:S(2)}) copy-start(bf16[96,768]{1,0:T(8,128)(2,1)} %reshape.341) | copy-start | bytes 442372
  323.3 7.5 %copy-start.50 = (s32[3]{0:T(128)S(1)}, s32[3]{0:T(128)}, u32[]{:S(2)}) copy-start(s32[3]{0:T(128)} %param.20) | copy-start | bytes 40
  327.6 45.6 %copy-start.27 = (bf16[3,768]{1,0:T(4,128)(2,1)S(1)}, bf16[3,768]{1,0:T(4,128)(2,1)}, u32[]{:S(2)}) copy-start(bf16[3,768]{1,0:T(4,128)(2,1)} %param.21) | copy-start | bytes 13828
  327.6 45.6 %copy-start.44 = (f32[3]{0:T(128)S(1)}, f32[3]{0:T(128)}, u32[]{:S(2)}) copy-start(f32[3]{0:T(128)} %copy-done.43) | copy-start | bytes 40
  327.6 84.7 %copy-start.21 = (bf16[3,196,768]{2,1,0:T(8,128)(2,1)S(1)}, bf16[3,196,768]{2,1,0:T(8,128)(2,1)}, u32[]{:S(2)}) copy-start(bf16[3,196,768]{2,1,0:T(8,128)(2,1)} %param.35) | copy-start | bytes 2709508
  327.6 84.7 %copy-start.33 = (f32[3,196]{1,0:T(4,128)S(1)}, f32[3,196]{1,0:T(4,128)}, u32[]{:S(2)}) copy-start(f32[3,196]{1,0:T(4,128)} %copy-done.32) | copy-start | bytes 7060
  332.9 40.2 %copy-start.48 = (f32[96]{0:T(128)}, f32[96]{0:T(128)S(1)}, u32[]{:S(2)}) copy-start(f32[96]{0:T(128)S(1)} %get-tuple-element.50) | copy-start | bytes 1156
  373.2 41.3 %copy-start.24 = (bf16[96,768]{1,0:T(8,128)(2,1)}, bf16[96,768]{1,0:T(8,128)(2,1)S(1)}, u32[]{:S(2)}) copy-start(bf16[96,768]{1,0:T(8,128)(2,1)S(1)} %reshape.343) | copy-start | bytes 442372
  373.5 37.8 %copy-start.46 = (f32[96,3]{0,1:T(4,128)}, f32[96,3]{0,1:T(4,128)S(1)}, u32[]{:S(2)}) copy-start(f32[96,3]{0,1:T(4,128)S(1)} %get-tuple-element.87) | copy-start | bytes 3460
  412.3 30.8 %slice-start.2 = ((s8[4718592]{0:T(1024)(128)(4,1)}), s8[524288]{0:T(1024)(128)(4,1)S(1)}, s32[]{:S(2)}) async-start(s8[4718592]{0:T(1024)(128)(4,1)} %bitcast.205), calls=%async_computation.2 | async-start | bytes 1048576
  414.7 28.4 %slice-start.3 = ((s8[4718592]{0:T(1024)(128)(4,1)}), s8[4194304]{0:T(1024)(128)(4,1)S(1)}, s32[]{:S(2)}) async-start(s8[4718592]{0:T(1024)(128)(4,1)} %bitcast.205), calls=%async_computation.3 | async-start | bytes 8388608
  424.9 18.2 %copy-start.12 = (f32[588,768]{1,0:T(8,128)S(1)}, f32[588,768]{1,0:T(8,128)}, u32[]{:S(2)}) copy-start(f32[588,768]{1,0:T(8,128)} %copy-done.11) | copy-start | bytes 5419012
  470.4 11.1 %copy-start.2 = (f32[588,768]{1,0:T(8,128)}, f32[588,768]{1,0:T(8,128)S(1)}, u32[]{:S(2)}) copy-start(f32[588,768]{1,0:T(8,128)S(1)} %reshape.311) | copy-start | bytes 5419012
  485.6 9.7 %slice-start = ((s8[7372800]{0:T(1024)(128)(4,1)}), s8[3178496]{0:T(1024)(128)(4,1)S(1)}, s32[]{:S(2)}) async-start(s8[7372800]{0:T(1024)(128)(4,1)} %bitcast.196), calls=%async_computation | async-start | bytes 6356992
  490.0 5.4 slice-start.1
  490.0 5.4 copy-start.16
  490.0 5.4 copy-start.17
  498.4 2.9 copy-start.7
  498.4 4.2 copy-start.9
  508.6 15.5 %copy-start.29 = (f32[768]{0:T(1024)S(1)}, f32[768]{0:T(1024)}, u32[]{:S(2)}) copy-start(f32[768]{0:T(1024)} %copy-done.28) | copy-start | bytes 9220
  514.1 10.0 %copy-start.14 = (f32[588,768]{1,0:T(8,128)S(1)}, f32[588,768]{1,0:T(8,128)}, u32[]{:S(2)}) copy-start(f32[588,768]{1,0:T(8,128)} %reshape.315) | copy-start | bytes 5419012
  514.1 10.0 %copy-start.36 = (f32[588]{0:T(1024)S(1)}, f32[588]{0:T(1024)}, u32[]{:S(2)}) copy-start(f32[588]{0:T(1024)} %div.92) | copy-start | bytes 7060
  514.1 10.0 %copy-start.37 = (f32[588]{0:T(1024)S(1)}, f32[588]{0:T(1024)}, u32[]{:S(2)}) copy-start(f32[588]{0:T(1024)} %rsqrt.50) | copy-start | bytes 7060
  524.1 5.9 copy-start.31
  524.1 6.6 copy-start.3
  524.1 6.6 copy-start.4
  530.0 1.8 copy-start.19
  530.0 2.1 copy-start.22
  531.1 4.1 copy-start.20
  548.4 82.1 %copy-start.34 = (f32[1536]{0:T(1024)S(1)}, f32[1536]{0:T(1024)}, u32[]{:S(2)}) copy-start(f32[1536]{0:T(1024)} %pad_maximum_fusion.5) | copy-start | bytes 18436
  548.4 82.1 %copy-start.35 = (f32[768]{0:T(1024)S(1)}, f32[768]{0:T(1024)}, u32[]{:S(2)}) copy-start(f32[768]{0:T(1024)} %get-tuple-element.46) | copy-start | bytes 9220
  548.4 82.1 %copy-start.38 = (f32[768]{0:T(1024)S(1)}, f32[768]{0:T(1024)}, u32[]{:S(2)}) copy-start(f32[768]{0:T(1024)} %get-tuple-element.42) | copy-start | bytes 9220
  548.4 82.1 %copy-start.39 = (f32[3072]{0:T(1024)S(1)}, f32[3072]{0:T(1024)}, u32[]{:S(2)}) copy-start(f32[3072]{0:T(1024)} %get-tuple-element.44) | copy-start | bytes 36868
  548.4 82.1 %copy-start.41 = (f32[768]{0:T(1024)S(1)}, f32[768]{0:T(1024)}, u32[]{:S(2)}) copy-start(f32[768]{0:T(1024)} %get-tuple-element.16) | copy-start | bytes 9220
  548.4 82.1 %copy-start.42 = (f32[768]{0:T(1024)S(1)}, f32[768]{0:T(1024)}, u32[]{:S(2)}) copy-start(f32[768]{0:T(1024)} %get-tuple-element.20) | copy-start | bytes 9220
  548.4 82.1 %copy-start.49 = (f32[96]{0:T(128)S(1)}, f32[96]{0:T(128)}, u32[]{:S(2)}) copy-start(f32[96]{0:T(128)} %copy-done.48) | copy-start | bytes 1156
  548.4 126.9 %copy-start.25 = (bf16[96,768]{1,0:T(8,128)(2,1)S(1)}, bf16[96,768]{1,0:T(8,128)(2,1)}, u32[]{:S(2)}) copy-start(bf16[96,768]{1,0:T(8,128)(2,1)} %copy-done.24) | copy-start | bytes 442372
  548.4 126.9 %copy-start.47 = (f32[96,3]{0,1:T(4,128)S(1)}, f32[96,3]{0,1:T(4,128)}, u32[]{:S(2)}) copy-start(f32[96,3]{0,1:T(4,128)} %copy-done.46) | copy-start | bytes 3460
  548.5 128.6 %copy-start.45 = (f32[3]{0:T(128)S(1)}, f32[3]{0:T(128)}, u32[]{:S(2)}) copy-start(f32[3]{0:T(128)} %copy-done.43) | copy-start | bytes 40

commit v2 on v0

v2 whole, which is shorter than its diff:
```python
import functools
import math

import jax
import jax.numpy as jnp
from jax import lax
from jax.experimental import pallas as pl
from jax.experimental.pallas import tpu as pltpu
from jax.sharding import PartitionSpec as P

MESH = pl.DeviceIdType.MESH
MIB = 1024 * 1024
GROUPS = 32
D = 768
HEADS = 12
PAD = 208
IMG = 3
TOK = IMG * PAD
QKV_ROWS, OUT_ROWS = 72, 24
ROWS = 96
VMEM_LIMIT = 63 * MIB
EPS = 1e-6
BF, F32 = jnp.bfloat16, jnp.float32


def dot(a, b):
    return lax.dot_general(a, b, (((1,), (0,)), ((), ())), preferred_element_type=F32)


def dot_nt(a, b):
    return lax.dot_general(a, b, (((1,), (1,)), ((), ())), preferred_element_type=F32)


def dot_exact(a, b, dims):
    return lax.dot_general(a, b, (dims, ((), ())), preferred_element_type=F32, precision=lax.Precision.HIGHEST)


def iota(shape, dim):
    return lax.broadcasted_iota(jnp.int32, shape, dim)


def split(numbers, by):
    quotient = jnp.floor((numbers.astype(F32) + 0.5) * (1.0 / by)).astype(jnp.int32)
    return quotient, numbers - quotient * by


class Pos:
    def __init__(p, F, r, n):
        p.F, p.r, p.n = F, r, n
        p.index = lax.axis_index("dp") * F + lax.axis_index("fsdp")
        p.g, p.rho = lax.div(p.index, r), lax.rem(p.index, r)
        p.c, p.z = lax.rem(p.g, 2), lax.rem(lax.div(p.g, 2), 4)
        p.x, p.y = lax.rem(lax.div(p.g, 8), 2), lax.div(p.g, 16)
        p.l = p.y + p.c * (p.x - p.y)
        p.f = p.x + p.c * (p.y - p.x)
        c, x, y, z = p.c, p.x, p.y, p.z
        p.sib = p.chip(y, x, z, 1 - c)
        p.fn = p.chip(y + c * (1 - 2 * y), x + (1 - c) * (1 - 2 * x), z, c)
        p.ln = p.chip(y + (1 - c) * (1 - 2 * y), x + c * (1 - 2 * x), z, c)
        p.up = p.chip(y, x, jnp.minimum(z + 1, 3), c)
        p.dn = p.chip(y, x, jnp.maximum(z - 1, 0), c)
        p.plane = lax.div(p.g, 2) * r + p.rho

    def device(p, linear):
        return (lax.div(linear, p.F), lax.rem(linear, p.F))

    def chip(p, y, x, z, c):
        return p.device((((y * 2 + x) * 4 + z) * 2 + c) * p.r + p.rho)

    def in_plane(p, q):
        return p.device((lax.div(q, p.r) * 2 + p.c) * p.r + lax.rem(q, p.r))

    def block(p, l, z, f):
        y, x = l + p.c * (f - l), f + p.c * (l - f)
        return p.chip(y, x, z, p.c)


def group_of(block):
    c = block // 16 if isinstance(block, int) else jnp.where(block >= 16, 1, 0)
    rest = block - c * 16
    if isinstance(block, int):
        l, z, f = rest // 8, rest // 2 % 4, rest % 2
    else:
        l = jnp.where(rest >= 8, 1, 0)
        zf = rest - 8 * l
        z = jnp.where(zf >= 2, 1, 0) + jnp.where(zf >= 4, 1, 0) + jnp.where(zf >= 6, 1, 0)
        f = zf - 2 * z
    y, x = l + c * (f - l), f + c * (l - f)
    return ((y * 2 + x) * 4 + z) * 2 + c


def enter(p):
    bar = pltpu.get_barrier_semaphore()
    half = p.n // 2

    def greet(i, carry):
        pl.semaphore_signal(bar, inc=1, device_id=p.in_plane(lax.rem(p.plane + i, half)), device_id_type=MESH)
        return carry

    lax.fori_loop(1, half, greet, 0)
    pl.semaphore_signal(bar, inc=1, device_id=p.sib, device_id_type=MESH)
    pl.semaphore_wait(bar, half)


class Gather:
    def __init__(s, p, held, send, recv):
        s.p, s.held, s.send, s.recv = p, held, send, recv

    def cp(s, at, ks, kr, dev):
        ref = s.held.at[at]
        return pltpu.make_async_remote_copy(
            src_ref=ref, dst_ref=ref, send_sem=s.send.at[ks], recv_sem=s.recv.at[kr], device_id=dev, device_id_type=MESH
        )

    def first(s):
        p = s.p
        return s.cp((p.c, p.l, p.z, p.f), 0, 0, p.fn)

    def first_in(s):
        p = s.p
        return s.cp((p.c, p.l, p.z, 1 - p.f), 0, 0, p.fn)

    def f_of(s, b):
        return s.p.f + b * (1 - 2 * s.p.f)

    def up(s, zz, b):
        return s.cp((s.p.c, s.p.l, zz, s.f_of(b)), 1 + 2 * zz + b, 1 + 2 * zz + b, s.p.up)

    def dn(s, zz, b):
        return s.cp((s.p.c, s.p.l, zz, s.f_of(b)), 9 + 2 * zz + b, 1 + 2 * zz + b, s.p.dn)

    def last(s, zz):
        return s.cp((s.p.c, s.p.l, zz), 17 + zz, 9 + zz, s.p.ln)

    def last_in(s, zz):
        return s.cp((s.p.c, 1 - s.p.l, zz), 17 + zz, 9 + zz, s.p.ln)

    def core(s, l, zz):
        return s.cp((s.p.c, l, zz), 21 + 4 * l + zz, 13 + 4 * l + zz, s.p.sib)

    def core_in(s, l, zz):
        return s.cp((1 - s.p.c, l, zz), 21 + 4 * l + zz, 13 + 4 * l + zz, s.p.sib)

    def own(s, b):
        p = s.p
        if b:
            s.first_in().wait_recv()
        else:
            s.first().start()

        @pl.when(p.z < 3)
        def _():
            s.up(p.z, b).start()

        @pl.when(p.z > 0)
        def _():
            s.dn(p.z, b).start()

        if b:
            s.last(p.z).start()
            s.core(p.l, p.z).start()

    def line(s, h, b):
        p = s.p

        @pl.when(p.z - h >= 0)
        def _():
            zz = p.z - h
            s.up(zz, b).wait_recv()

            @pl.when(p.z < 3)
            def _():
                s.up(zz, b).start()

            if b:
                s.last(zz).start()
                s.core(p.l, zz).start()

        @pl.when(p.z + h <= 3)
        def _():
            zz = p.z + h
            s.dn(zz, b).wait_recv()

            @pl.when(p.z > 0)
            def _():
                s.dn(zz, b).start()

            if b:
                s.last(zz).start()
                s.core(p.l, zz).start()

    def arrive(s, h):
        p = s.p

        def one(zz):
            s.last_in(zz).wait_recv()
            s.core(1 - p.l, zz).start()

        if h == 0:
            one(p.z)
        else:

            @pl.when(p.z - h >= 0)
            def _():
                one(p.z - h)

            @pl.when(p.z + h <= 3)
            def _():
                one(p.z + h)

    def finish(s):
        for zz in range(4):
            for l in range(2):
                s.core_in(l, zz).wait_recv()

    def drain(s):
        p = s.p
        s.first().wait_send()
        for zz in range(4):

            @pl.when((p.z < 3) & (zz <= p.z))
            def _():
                s.up(zz, 0).wait_send()
                s.up(zz, 1).wait_send()

            @pl.when((p.z > 0) & (zz >= p.z))
            def _():
                s.dn(zz, 0).wait_send()
                s.dn(zz, 1).wait_send()

            s.last(zz).wait_send()
            for l in range(2):
                s.core(l, zz).wait_send()


class Scatter:
    def __init__(s, p, sums, room, ends, send, recv):
        s.p, s.sums, s.room, s.ends, s.send, s.recv = p, sums, room, ends, send, recv

    def cp(s, src, dst, ks, kr, dev):
        return pltpu.make_async_remote_copy(
            src_ref=src, dst_ref=dst, send_sem=s.send.at[ks], recv_sem=s.recv.at[kr], device_id=dev, device_id_type=MESH
        )

    def core_cp(s, l):
        return s.cp(s.sums.at[1 - s.p.c, l], s.room(l), 1 + l, 1 + l, s.p.sib)

    def side_cp(s, zz):
        return s.cp(s.sums.at[s.p.c, 1 - s.p.l, zz], s.room(2).at[zz], 3 + zz, 3 + zz, s.p.ln)

    def f_of(s, b):
        return 1 - s.p.f if b == 0 else s.p.f

    def here(s, zz, b):
        return s.sums.at[s.p.c, s.p.l, zz, s.f_of(b)]

    def up_far(s, zz, b):
        return s.cp(s.here(zz, b), s.room(3).at[zz, b], 7 + 2 * zz + b, 7 + 2 * zz + b, s.p.up)

    def up_end(s, zz, b):
        return s.cp(s.here(zz, b), s.ends.at[b], 7 + 2 * zz + b, 15 + b, s.p.up)

    def down(s, zz, b):
        return s.cp(s.here(zz, b), s.room(3).at[zz, b], 15 + 2 * zz + b, 7 + 2 * zz + b, s.p.dn)

    def last_cp(s):
        return s.cp(s.here(s.p.z, 0), s.ends.at[2], 0, 0, s.p.fn)

    def core_send(s, l):
        s.core_cp(l).start()

    def core_add(s, l):
        s.core_cp(l).wait_recv()
        room = s.room(l)

        def body(zz, carry):
            for f in range(2):
                ref = s.sums.at[s.p.c, l, zz, f]
                ref[...] = (ref[...].astype(F32) + room[zz, f].astype(F32)).astype(BF)
            return carry

        lax.fori_loop(0, 4, body, 0)

    def add(s, zz, b, ref):
        total = s.here(zz, b)
        total[...] = (total[...].astype(F32) + ref[...].astype(F32)).astype(BF)

    def by_distance(s, h, fn):
        p = s.p
        if h == 0:
            fn(p.z)
            return

        @pl.when(p.z + h <= 3)
        def _():
            fn(p.z + h)

        @pl.when(p.z - h >= 0)
        def _():
            fn(p.z - h)

    def side_send(s):
        for h in (3, 2, 1, 0):
            s.by_distance(h, lambda zz: s.side_cp(zz).start())

    def side_add(s, h):
        def one(zz):
            s.side_cp(zz).wait_recv()
            for f in (0, 1):
                total = s.sums.at[s.p.c, s.p.l, zz, f]
                total[...] = (total[...].astype(F32) + s.room(2)[zz, f].astype(F32)).astype(BF)

        s.by_distance(h, one)

    def line(s, h, b):
        p = s.p
        if h > 0:

            @pl.when(p.z + h <= 3)
            def _():
                zz = p.z + h

                @pl.when(p.z > 0)
                def _():
                    s.up_far(zz, b).wait_recv()
                    s.add(zz, b, s.room(3).at[zz, b])

                if h == 1:
                    s.up_end(zz, b).start()
                else:
                    s.up_far(zz, b).start()

            @pl.when(p.z - h >= 0)
            def _():
                zz = p.z - h

                @pl.when(p.z < 3)
                def _():
                    s.down(zz, b).wait_recv()
                    s.add(zz, b, s.room(3).at[zz, b])

                s.down(zz, b).start()

        else:

            @pl.when(p.z > 0)
            def _():
                s.up_end(p.z, b).wait_recv()
                s.add(p.z, b, s.ends.at[b])

            @pl.when(p.z < 3)
            def _():
                s.down(p.z, b).wait_recv()
                s.add(p.z, b, s.room(3).at[p.z, b])

            if b == 0:
                s.last_cp().start()

    def final(s):
        s.last_cp().wait_recv()
        return s.here(s.p.z, 1)[...].astype(F32) + s.ends[2].astype(F32)

    def drain(s):
        p = s.p
        for l in range(2):
            s.core_cp(l).wait_send()
        for zz in range(4):
            s.side_cp(zz).wait_send()

            @pl.when(zz > p.z)
            def _():
                s.up_far(zz, 0).wait_send()
                s.up_far(zz, 1).wait_send()

            @pl.when(zz < p.z)
            def _():
                s.down(zz, 0).wait_send()
                s.down(zz, 1).wait_send()

        s.last_cp().wait_send()


def qkv_runs(start, stop):
    runs, row = [], start
    while row < stop:
        chip, inside = divmod(row, 2 * QKV_ROWS)
        z, x, y = chip % 4, chip // 4 % 2, chip // 8
        first = inside < ROWS
        until = min(stop, chip * 2 * QKV_ROWS + (ROWS if first else 2 * QKV_ROWS))
        low = inside if first else inside - ROWS
        at = (0, y, z, x) if first else (1, x, z, y)
        runs.append((at, low, low + until - row))
        row = until
    return runs


def out_runs(start, stop):
    runs, row = [], start
    while row < stop:
        chip, inside = divmod(row, 2 * OUT_ROWS)
        z, x, y = chip % 4, chip // 4 % 2, chip // 8
        until = min(stop, (chip + 1) * 2 * OUT_ROWS)
        low = inside + 2 * (QKV_ROWS - OUT_ROWS) // 2
        runs.append(((1, x, z, y), low, low + until - row))
        row = until
    return runs


def load_runs(ref, runs, lanes=slice(None)):
    return jnp.concatenate([ref[at + (slice(a, b), lanes)] for at, a, b in runs], 0)


def store_runs(ref, runs, value):
    row = 0
    for at, a, b in runs:
        ref[at + (slice(a, b), slice(None))] = value[row : row + b - a]
        row += b - a


def slabs(ref, first, count):
    return jnp.concatenate([ref[first + k] for k in range(count)], 1)


def norm_parts(values):
    centered = values - jnp.mean(values, -1, keepdims=True)
    inverse = lax.rsqrt(jnp.mean(centered * centered, -1, keepdims=True) + EPS)
    return centered * inverse, inverse


def norm_grad(grad, gain, normalized, inverse):
    h = grad * gain
    return (h - jnp.mean(h, -1, keepdims=True) - normalized * jnp.mean(h * normalized, -1, keepdims=True)) * inverse


def gelu_parts(x):
    z = jnp.abs(x) * math.sqrt(0.5)
    under = 1.0 + 0.3275911 * z
    t = pl.reciprocal(under, approx=True)
    t = t * (2.0 - under * t)
    bell = jnp.exp(-0.5 * x * x)
    poly = ((((1.061405429 * t - 1.453152027) * t + 1.421413741) * t - 0.284496736) * t + 0.254829592) * t
    tail = 0.5 * poly * bell
    cdf = jnp.where(x >= 0, 1.0 - tail, tail)
    return x * cdf, cdf + x * bell * (1.0 / math.sqrt(2.0 * math.pi))


CUTS = ((0, 48), (48, 48), (96, 48), (144, 64))


def by_rows(fn):
    def body(i, carry):
        for start, size in CUTS:
            fn(i, pl.ds(pl.multiple_of(i * PAD + start, 16), size))
        return carry

    lax.fori_loop(0, IMG, body, 0)


def layer_kernel(
    F,
    r,
    n,
    qo_ref,
    f1_ref,
    f2_ref,
    small_ref,
    img_ref,
    cot_ref,
    mask_ref,
    text_ref,
    scale_ref,
    mix_ref,
    res_ref,
    loss_ref,
    tg_ref,
    dqo_ref,
    df1_ref,
    df2_ref,
    dvec_ref,
    W,
    G,
    room,
    ends,
    small,
    swap_grad,
    norm1,
    qkv,
    att,
    lse,
    sec,
    act,
    slope,
    grad2,
    temp,
    vec,
    vec_grad,
    pooled,
    row_grad,
    pair_rows,
    units,
    vec_out,
    vec_core,
    vec_in,
    g_send,
    g_recv,
    s_send,
    s_recv,
    misc,
    credit,
):
    p = Pos(F, r, n)
    half = n // 2
    total = IMG * n
    per_group = IMG * r
    small_rows = small.shape[4]
    qo_g, f1_g, f2_g = (Gather(p, W.at[m], g_send.at[m], g_recv.at[m]) for m in range(3))
    sm_g = Gather(p, small, g_send.at[3], g_recv.at[3])

    def remote(src, dst, k, dev):
        return pltpu.make_async_remote_copy(
            src_ref=src, dst_ref=dst, send_sem=misc.at[2 * k], recv_sem=misc.at[2 * k + 1], device_id=dev, device_id_type=MESH
        )

    W[1, p.c, p.l, p.z, p.f] = f1_ref[...]
    W[2, p.c, p.l, p.z, p.f] = f2_ref[...]
    small[p.c, p.l, p.z, p.f] = small_ref[...]
    vec_grad[...] = jnp.zeros(vec_grad.shape, F32)
    enter(p)
    swap_copy = remote(qo_ref.at[1 - p.c], G.at[0, 0, 0, 0, 0], 0, p.sib)
    swap_copy.start()
    sm_g.own(0)
    f1_early = False
    swap_copy.wait_recv()
    W[0, p.c, p.l, p.z, p.f] = (qo_ref[p.c].astype(F32) + G[0, 0, 0, 0, 0].astype(F32)).astype(BF)
    qo_g.own(0)
    sm_g.own(1)
    qo_g.own(1)
    sm_g.line(1, 0)
    sm_g.line(1, 1)
    sm_g.arrive(0)
    qo_g.line(1, 0)
    sm_g.line(2, 0)
    sm_g.line(2, 1)
    sm_g.arrive(1)
    qo_g.line(1, 1)
    qo_g.arrive(0)
    sm_g.line(3, 0)
    sm_g.line(3, 1)
    sm_g.arrive(2)
    sm_g.arrive(3)
    sm_g.finish()


    def picked(k):
        source, target = iota((GROUPS, GROUPS * small_rows), 1), iota((GROUPS, GROUPS * small_rows), 0)
        return dot(jnp.where(source == target * small_rows + k, 1.0, 0.0).astype(BF), small[...].reshape(GROUPS * small_rows, 128)).astype(BF)

    table = [(0, 0, 24, 0), (0, 24, 24, 0), (0, 48, 24, 0), (0, 72, 24, 0), (0, 96, 24, 0), (1, 0, 24, 0), (1, 24, 48, 0), (1, 24, 48, D)]
    table += [(2, 0, 96, D * q) for q in range(4)]

    def spread(k, offset, width, base):
        owner, inside = split(iota((1, D), 1) + base, width)
        names = iota((GROUPS, 1), 0)
        names = names if k == 2 else group_of(names)
        mask = jnp.where(names == owner, 1.0, 0.0)
        places = jnp.where(iota((128, D), 0) == inside + offset, 1.0, 0.0)
        return mask, places

    @pl.when(p.index >= 0)
    def _():
      message_rows = [picked(k) for k in range(3)]
      for row, (k, offset, width, base) in enumerate(table):
        mask, places = spread(k, offset, width, base)
        vec[row : row + 1, :] = jnp.sum(mask * dot(message_rows[k], places.astype(BF)), 0, keepdims=True)

    def first_norm(i, rows):
        normalized, _ = norm_parts(img_ref[rows].astype(F32))
        norm1[rows] = (normalized * vec[0:1] + vec[1:2]).astype(BF)

    by_rows(first_norm)
    qo_g.line(2, 0)
    qo_g.line(2, 1)
    f1_g.own(0)
    qo_g.arrive(1)
    f1_g.own(1)
    qo_g.line(3, 0)
    qo_g.line(3, 1)
    qo_g.arrive(2)
    qo_g.arrive(3)
    qo_g.finish()

    for j in range(9):
        part = dot_nt(norm1[...], load_runs(W.at[0], qkv_runs(256 * j, 256 * j + 256)))
        if j < 3:
            part = part + vec[6:7, 256 * j : 256 * j + 256]
        elif j >= 6:
            part = part + vec[7:8, 256 * (j - 6) : 256 * (j - 6) + 256]
        part = part.astype(BF)
        qkv[2 * j] = part[:, :128]
        qkv[2 * j + 1] = part[:, 128:]
        if j == 2:
            f1_g.line(1, 0)
            f1_g.line(1, 1)
            f1_g.arrive(0)
        if j == 6:
            f1_g.line(2, 0)
            f1_g.line(2, 1)
            f2_g.own(0)
            f1_g.arrive(1)
            f2_g.own(1)

    low = iota((1, 128), 1) < 64

    def halves(value):
        zero = jnp.zeros_like(value)
        return jnp.where(low, value, zero), jnp.where(low, zero, value)

    def head_pair(i, pair):
        rows = pl.ds(pl.multiple_of(i * PAD, 16), PAD)
        return rows, qkv[pair, rows], qkv[6 + pair, rows], qkv[12 + pair, rows]

    def attend(it, carry):
        i, pair = lax.div(it, 6), lax.rem(it, 6)
        rows, q, k, v = head_pair(i, pair)
        v_t = v.T
        bars = jnp.concatenate([jnp.where(mask_ref[rows] > 0, 0.0, -1e30)] * 2, 1)[:, :PAD]
        parts = []
        for h, k_h in enumerate(halves(k * jnp.asarray(0.125, BF))):
            scores = dot_nt(k_h, q) + bars
            top = jnp.max(scores, 0, keepdims=True)
            terms = jnp.exp(scores - top)
            amount = jnp.sum(terms, 0, keepdims=True)
            lse[it * 2 + h] = top + jnp.log(amount)
            parts.append(dot(v_t[64 * h : 64 * h + 64], terms.astype(BF)) * (1.0 / amount))
        att[pair, rows] = jnp.concatenate(parts, 0).T.astype(BF)
        return carry

    lax.fori_loop(0, 4, attend, 0)
    f1_g.line(3, 0)
    f1_g.line(3, 1)
    f1_g.arrive(2)
    lax.fori_loop(4, 8, attend, 0)
    f1_g.arrive(3)
    f2_g.line(1, 0)
    f2_g.line(1, 1)
    f2_g.arrive(0)
    lax.fori_loop(8, 14, attend, 0)
    f2_g.line(2, 0)
    f2_g.line(2, 1)
    f2_g.arrive(1)
    lax.fori_loop(14, 18, attend, 0)

    attended = slabs(att, 0, 6)
    for j in range(3):
        lanes = slice(256 * j, 256 * j + 256)
        part = dot_nt(attended, load_runs(W.at[0], out_runs(256 * j, 256 * j + 256)))
        res_ref[:, lanes] = img_ref[:, lanes].astype(F32) + part + vec[2:3, lanes]

    def second_norm(i, rows):
        normalized, _ = norm_parts(res_ref[rows])
        value = (normalized * vec[3:4] + vec[4:5]).astype(BF)
        for k in range(6):
            sec[k, rows] = value[:, 128 * k : 128 * k + 128]

    by_rows(second_norm)
    f1_g.finish()

    def image_rows(i):
        return pl.ds(pl.multiple_of(i * PAD, 16), PAD)

    def expand(it, carry):
        q, rows = lax.div(it, IMG), image_rows(lax.rem(it, IMG))
        left = jnp.concatenate([sec[k, rows] for k in range(6)], 1)
        pre = dot_nt(left, W[1, lax.div(q, 2), lax.rem(q, 2)].reshape(D, D)) + vec[pl.ds(8 + q, 1), :]
        value, derivative = gelu_parts(pre)
        act[q, rows] = value.astype(BF)
        slope[q, rows] = derivative.astype(BF)
        return carry

    lax.fori_loop(0, 3, expand, 0)
    f2_g.line(3, 0)
    f2_g.line(3, 1)
    f2_g.arrive(2)
    lax.fori_loop(3, 9, expand, 0)
    f2_g.arrive(3)
    lax.fori_loop(9, 12, expand, 0)
    f2_g.finish()

    def contract(hidden_units, m):
        def body(i, carry):
            rows = image_rows(i)
            for j in range(3):
                lanes = slice(256 * j, 256 * j + 256)
                left = jnp.concatenate([hidden_units[q, rows] for q in range(4)], 1)
                temp[rows, lanes] = dot(left, W[m, :, :, :, :, :, lanes].reshape(4 * D, 256))
            return carry

        lax.fori_loop(0, IMG, body, 0)

    contract(act, 2)

    def wide(column):
        return jnp.concatenate([column] * 6, 1)

    pooled[...] = jnp.zeros(pooled.shape, F32)
    for i in range(IMG):
        sums, count = jnp.zeros((1, D), F32), jnp.zeros((1, 128), F32)
        for start, size in CUTS:
            rows = pl.ds(i * PAD + start, size)
            mask = mask_ref[rows]
            outputs = (res_ref[rows] + temp[rows] + vec[5:6]) * wide(mask)
            mix_ref[rows] = outputs.astype(BF)
            sums = sums + jnp.sum(outputs, 0, keepdims=True)
            count = count + jnp.sum(mask, 0, keepdims=True)
        pooled[i : i + 1, :] = sums / wide(count)
        pooled[8 + i : 9 + i, :] = wide(count)

    def unit(values):
        inverse = lax.rsqrt(jnp.sum(values * values, -1, keepdims=True) + EPS)
        return values * inverse, inverse

    def unit_grad(grad, values, inverse):
        return inverse * grad - inverse * inverse * inverse * values * jnp.sum(values * grad, -1, keepdims=True)

    own_pooled = pooled[0:8]
    image_unit, image_inverse = unit(own_pooled)
    image_unit = image_unit.astype(BF)
    message = jnp.zeros((32, 128), F32)
    for k in range(6):
        at = jnp.where((iota((32, 8), 0) == iota((32, 8), 1) + IMG * k) & (iota((32, 8), 1) < IMG), 1.0, 0.0).astype(BF)
        message = message + dot(at, image_unit[:, 128 * k : 128 * k + 128])
    units[p.c, p.plane] = message.astype(BF)

    def push(i, carry):
        q = lax.rem(p.plane + i, half)
        remote(units.at[p.c, p.plane], units.at[p.c, p.plane], 1, p.in_plane(q)).start()
        return carry

    lax.fori_loop(1, half, push, 0)
    all_but_own = remote(units.at[p.c, pl.ds(0, half - 1)], units.at[p.c, pl.ds(0, half - 1)], 1, p.sib)

    def gathered(source_chunks, chunk_rows, row_of, tiles, base):
        results = []
        for k in range(tiles):
            value = jnp.zeros((total, 128), F32)
            for number, chunk in source_chunks:
                owner, inside = split(iota((1, chunk_rows), 1), base)
                target = row_of(owner, inside, number, k)
                value = value + dot(jnp.where(iota((total, chunk_rows), 0) == target, 1.0, 0.0).astype(BF), chunk)
            results.append(value)
        return results

    def text_row(owner, inside, number, k):
        at = inside - 3 - per_group * k
        group = group_of(owner + 8 * number)
        return jnp.where((at >= 0) & (at < per_group), group * per_group + at, -1)

    chunks = [(2 * c + l, small[c, l].reshape(8 * small_rows, 128)) for c in range(2) for l in range(2)]
    tiles = gathered(chunks, 8 * small_rows, text_row, 7, small_rows)
    for b in range(r):
        for k in range(6):
            G[1, b // 16, b // 8 % 2, b // 2 % 4, b % 2, :, 128 * k : 128 * k + 128] = tiles[k][ROWS * b : ROWS * b + ROWS].astype(BF)

    def texts():
        return jnp.concatenate([G[1, b // 16, b // 8 % 2, b // 2 % 4, b % 2] for b in range(r)], 0)

    pair_rows[...] = tiles[6]

    all_but_own.wait_recv()
    share = remote(units.at[p.c], units.at[p.c], 2, p.sib)
    share.start()
    remote(units.at[1 - p.c], units.at[1 - p.c], 2, p.sib).wait_recv()

    for k in range(6):

        def add_chunk(number, value, k=k):
            c, at = lax.div(number * 16, half), lax.rem(number * 16, half)
            owner, inside = split(iota((1, 512), 1), 32)
            q = owner + at
            t = inside - IMG * k
            if r == 1:
                linear = 2 * q + c
            else:
                chip, rho = split(q, r)
                linear = (2 * chip + c) * r + rho
            target = jnp.where((t >= 0) & (t < IMG), linear * IMG + t, -1)
            pick = jnp.where(iota((total, 512), 0) == target, 1.0, 0.0).astype(BF)
            return value + dot(pick, units[c, pl.ds(at, 16)].reshape(512, 128))

        value = lax.fori_loop(0, n // 16, add_chunk, jnp.zeros((total, 128), F32)).astype(BF)
        for b in range(r):
            G[2, b // 16, b // 8 % 2, b // 2 % 4, b % 2, :, 128 * k : 128 * k + 128] = value[ROWS * b : ROWS * b + ROWS]

    def block(m, b):
        return G[m, lax.div(b, 16), lax.rem(lax.div(b, 8), 2), lax.rem(lax.div(b, 2), 4), lax.rem(b, 2)]

    scale = scale_ref[0:1, 0:1]
    row = jnp.zeros((1, total), F32)

    def similar(b, col_top):
        rows = pl.ds(pl.multiple_of(b * ROWS, ROWS), ROWS)
        part = dot_nt(block(2, b), texts()) * scale
        temp[rows, :total] = part
        return jnp.maximum(col_top, jnp.max(part, 0, keepdims=True))

    col_top = lax.fori_loop(0, r, similar, row - jnp.inf)

    def by_blocks(fn):
        def body(b, carry):
            rows = pl.ds(pl.multiple_of(b * ROWS, ROWS), ROWS)
            part = temp[rows, :total]
            top = jnp.max(part, 1, keepdims=True)
            row_lse = top + jnp.log(jnp.sum(jnp.exp(part - top), 1, keepdims=True))
            match = jnp.where(iota((ROWS, total), 1) == pair_of(rows), 1.0, 0.0)
            return fn(b, part, row_lse, match, carry)

        return body

    def pair_of(rows):
        column = pair_rows[rows]
        return (column[:, 0:1] * 256.0 + column[:, 1:2]).astype(jnp.int32)

    def sums(b, part, row_lse, match, carry):
        col_sum, loss = carry
        paired = jnp.sum(jnp.sum(part * match, 1, keepdims=True), 0, keepdims=True)
        return col_sum + jnp.sum(jnp.exp(part - col_top), 0, keepdims=True), loss + jnp.sum(row_lse, 0, keepdims=True) - 2.0 * paired

    col_sum, loss = lax.fori_loop(0, r, by_blocks(sums), (row, jnp.zeros((1, 1), F32)))
    col_lse = col_top + jnp.log(col_sum)
    loss = (loss + jnp.sum(col_lse, 1, keepdims=True)) / (2.0 * total)
    loss_ref[...] = jnp.broadcast_to(loss, (8, 128))

    def own_of(places):
        return jnp.where((places == iota(places.shape, 0) + IMG * p.index) & (iota(places.shape, 0) < IMG), 1.0, 0.0).astype(BF)

    own = own_of(iota((8, total), 1))

    def similar_grad(b, part, row_lse, match, carry):
        grad_rows, grad_text = carry
        grad = 0.5 * (jnp.exp(part - row_lse) + jnp.exp(part - col_lse)) - match
        grad = (scale * grad).astype(BF)
        own_rows = own_of(iota((8, ROWS), 1) + b * ROWS)
        return grad_rows + dot(own_rows, grad), grad_text + dot(dot_nt(own, grad).astype(BF), block(2, b))

    grad_rows, grad_text = lax.fori_loop(0, r, by_blocks(similar_grad), (jnp.zeros((8, total), F32), jnp.zeros((8, D), F32)))
    grad_unit = dot(grad_rows.astype(BF), texts())
    row_grad[...] = unit_grad(grad_unit, own_pooled, image_inverse) / jnp.maximum(pooled[8:16], 1.0)
    text_rows = text_ref[...]
    _, text_inverse = unit(text_rows)
    tg_ref[...] = unit_grad(grad_text, text_rows, text_inverse)

    sc0, sc1, sc2 = (
        Scatter(p, G.at[m], area, ends.at[1 if m == 1 else 0], s_send.at[m], s_recv.at[m])
        for m, area in (
            (0, lambda k: room.at[k]),
            (1, lambda k: W.at[2, k // 2, k % 2] if isinstance(k, int) else W.at[2, 0, k]),
            (2, lambda k: room.at[k]),
        )
    )

    def out_grad(i, rows):
        return wide(mask_ref[rows]) * (cot_ref[rows].astype(F32) + row_grad[pl.ds(i, 1), :])

    def first_round(i, rows):
        value = out_grad(i, rows).astype(BF)
        grad2[rows] = value
        vec_grad[5:6] += jnp.sum(value.astype(F32), 0, keepdims=True)

    by_rows(first_round)
    order = ((1 - p.c, 1 - p.f), (p.c, 1 - p.l), (1 - p.c, p.f), (p.c, p.l))

    def weight_grad(m, at, left, right):
        left = left.T
        for j in range(3):
            lanes = slice(256 * j, 256 * j + 256)
            G[(m,) + at + (slice(None), slice(None), slice(None), lanes)] = (
                dot(left, right[:, lanes]).astype(BF).reshape(4, 2, ROWS, 256)
            )

    for step, at in enumerate(order):
        weight_grad(2, at, act[2 * at[0] + at[1]], grad2[...])
        if step == 0:
            sc2.core_send(1 - p.f)
        if step == 1:
            sc2.core_add(1 - p.l)
            sc2.side_send()
        if step == 2:
            sc2.core_send(p.f)
    sc2.core_add(p.l)
    sc2.side_add(3)
    sc2.line(3, 0)
    sc2.line(3, 1)
    for q in range(4):

        def back(i, carry, q=q):
            rows = image_rows(i)
            value = dot_nt(grad2[rows], W[2, q // 2, q % 2].reshape(D, D)) * slope[q, rows].astype(F32)
            value = value.astype(BF)
            slope[q, rows] = value
            vec_grad[8 + q : 9 + q] += jnp.sum(value.astype(F32), 0, keepdims=True)
            return carry

        lax.fori_loop(0, IMG, back, 0)
        if q == 1:
            sc2.side_add(2)
            sc2.line(2, 0)
            sc2.line(2, 1)
    f2_g.drain()
    line_up, line_down = p.z < 3, p.z > 0

    def give(k):
        pl.semaphore_signal(credit.at[k], inc=1, device_id=p.sib, device_id_type=MESH)
        pl.semaphore_signal(credit.at[k + 1], inc=1, device_id=p.ln, device_id_type=MESH)
        pl.semaphore_signal(credit.at[k + 4], inc=1, device_id=p.fn, device_id_type=MESH)

        @pl.when(line_down)
        def _():
            pl.semaphore_signal(credit.at[k + 2], inc=1, device_id=p.dn, device_id_type=MESH)

        @pl.when(line_up)
        def _():
            pl.semaphore_signal(credit.at[k + 3], inc=1, device_id=p.up, device_id_type=MESH)

    def take_line(k):
        pl.semaphore_wait(credit.at[k + 4], 1)

        @pl.when(line_up)
        def _():
            pl.semaphore_wait(credit.at[k + 2], 1)

        @pl.when(line_down)
        def _():
            pl.semaphore_wait(credit.at[k + 3], 1)

    give(0)
    for step, at in enumerate(order):
        weight_grad(1, at, slope[2 * at[0] + at[1]], slabs(sec, 0, 6))
        if step == 0:
            pl.semaphore_wait(credit.at[0], 1)
            sc1.core_send(1 - p.f)
            sc2.side_add(1)
            sc2.line(1, 0)
            sc2.line(1, 1)
        if step == 1:
            sc1.core_add(1 - p.l)
            pl.semaphore_wait(credit.at[1], 1)
            sc1.side_send()
        if step == 2:
            sc1.core_send(p.f)
    sc1.core_add(p.l)
    sc2.side_add(0)
    sc2.line(0, 0)
    sc2.line(0, 1)
    take_line(0)
    sc1.side_add(3)
    sc1.line(3, 0)
    sc1.line(3, 1)
    contract(slope, 1)
    df2_ref[...] = sc2.final()
    give(5)

    def second_back(i, rows):
        grad = temp[rows]
        normalized, inverse = norm_parts(res_ref[rows])
        total_grad = out_grad(i, rows) + norm_grad(grad, vec[3:4], normalized, inverse)
        res_ref[rows] = total_grad
        rounded = total_grad.astype(BF)
        grad2[rows] = rounded
        vec_grad[3:4] += jnp.sum(grad * normalized, 0, keepdims=True)
        vec_grad[4:5] += jnp.sum(grad, 0, keepdims=True)
        vec_grad[2:3] += jnp.sum(rounded.astype(F32), 0, keepdims=True)

    by_rows(second_back)
    sc1.side_add(2)
    sc1.line(2, 0)
    sc1.line(2, 1)
    attended = slabs(att, 0, 6)
    for j in range(3):
        lanes = slice(256 * j, 256 * j + 256)
        store_runs(G.at[0], out_runs(256 * j, 256 * j + 256), dot(grad2[:, lanes].T, attended).astype(BF))
    for j in range(3):
        lanes = slice(256 * j, 256 * j + 256)
        part = dot(grad2[...], load_runs(W.at[0], out_runs(0, D), lanes)).astype(BF)
        sec[2 * j] = part[:, :128]
        sec[2 * j + 1] = part[:, 128:]

    def attend_back(it, carry):
        i, pair = lax.div(it, 6), lax.rem(it, 6)
        rows, q, k, v = head_pair(i, pair)
        grad_out = sec[pair, rows]
        q, k = q * jnp.asarray(0.125, BF), k * jnp.asarray(0.125, BF)
        k_t = k.T
        bars = jnp.concatenate([jnp.where(mask_ref[rows] > 0, 0.0, -1e30)] * 2, 1)[:, :PAD]
        q_halves, out_halves, v_halves = halves(q), halves(grad_out), halves(v)
        plain_q = qkv[pair, rows]
        grad_v, grad_k, grad_q = 0.0, 0.0, []
        for h, k_h in enumerate(halves(k)):
            scores = dot_nt(k_h, plain_q) + bars
            probs = jnp.exp(scores - lse[it * 2 + h])
            grad_v = grad_v + dot(probs.astype(BF), out_halves[h])
            grad_probs = dot_nt(v_halves[h], grad_out)
            grad_scores = (probs * (grad_probs - jnp.sum(grad_probs * probs, 0, keepdims=True))).astype(BF)
            grad_k = grad_k + dot(grad_scores, q_halves[h])
            grad_q.append(dot(k_t[64 * h : 64 * h + 64], grad_scores))
        qkv[pair, rows] = jnp.concatenate(grad_q, 0).T.astype(BF)
        qkv[6 + pair, rows] = grad_k.astype(BF)
        qkv[12 + pair, rows] = grad_v.astype(BF)
        return carry

    lax.fori_loop(0, 6, attend_back, 0)
    sc1.side_add(1)
    sc1.line(1, 0)
    sc1.line(1, 1)
    lax.fori_loop(6, 14, attend_back, 0)
    sc1.side_add(0)
    sc1.line(0, 0)
    sc1.line(0, 1)
    lax.fori_loop(14, 18, attend_back, 0)
    for j in range(9):
        left = slabs(qkv, 2 * j, 2)
        store_runs(G.at[0], qkv_runs(256 * j, 256 * j + 256), dot(left.T, norm1[...]).astype(BF))
        if j < 3 or j >= 6:
            row, lanes = (6, slice(256 * j, 256 * j + 256)) if j < 3 else (7, slice(256 * (j - 6), 256 * (j - 6) + 256))
            vec_grad[row : row + 1, lanes] = jnp.sum(left.astype(F32), 0, keepdims=True)
    pl.semaphore_wait(credit.at[5], 1)
    sc0.core_send(1 - p.f)
    sc0.core_send(p.f)
    sc0.core_add(1 - p.l)
    pl.semaphore_wait(credit.at[6], 1)
    sc0.side_send()
    sc0.core_add(p.l)
    df1_ref[...] = sc1.final()
    take_line(5)
    sc0.side_add(3)
    sc0.line(3, 0)
    sc0.line(3, 1)

    def contract_joined(i, carry):
        rows = image_rows(i)
        for j in range(3):
            lanes = slice(256 * j, 256 * j + 256)
            left = jnp.concatenate([qkv[k, rows] for k in range(18)], 1)
            temp[rows, lanes] = dot(left, load_runs(W.at[0], qkv_runs(0, 3 * D), lanes))
        return carry

    lax.fori_loop(0, IMG, contract_joined, 0)
    sc0.side_add(2)
    sc0.line(2, 0)
    sc0.line(2, 1)

    def first_back(i, rows):
        grad = temp[rows]
        normalized, inverse = norm_parts(img_ref[rows].astype(F32))
        res_ref[rows] += norm_grad(grad, vec[0:1], normalized, inverse)
        vec_grad[0:1] += jnp.sum(grad * normalized, 0, keepdims=True)
        vec_grad[1:2] += jnp.sum(grad, 0, keepdims=True)

    by_rows(first_back)
    sc0.side_add(1)
    sc0.line(1, 0)
    sc0.line(1, 1)

    @pl.when(p.index >= 0)
    def _():
      outgoing = jnp.zeros((GROUPS * 8, 128), F32)
      for k in range(3):
          rows_k = jnp.zeros((GROUPS, 128), F32)
          for row, (kk, offset, width, base) in enumerate(table):
              if kk == k:
                  mask, places = spread(k, offset, width, base)
                  rows_k = rows_k + dot_exact(mask * vec_grad[row : row + 1], places, ((1,), (1,)))
          at = jnp.where(iota((GROUPS * 8, GROUPS), 0) == 8 * iota((GROUPS * 8, GROUPS), 1) + k, 1.0, 0.0)
          outgoing = outgoing + dot_exact(at, rows_k, ((1,), (0,)))
      vec_out[...] = outgoing.reshape(2, 16, 8, 128)
    vec_swap = remote(vec_out.at[1 - p.c], vec_core, 3, p.sib)
    vec_swap.start()
    vec_swap.wait_recv()
    vec_out[p.c] += vec_core[...]
    mine = (p.l * 4 + p.z) * 2 + p.f

    def push_vec(i, carry):
        q = lax.rem(mine + i, 16)
        dev = p.block(lax.div(q, 8), lax.rem(lax.div(q, 2), 4), lax.rem(q, 2))
        remote(vec_out.at[p.c, q], vec_in.at[mine], 4, dev).start()
        return carry

    lax.fori_loop(1, 16, push_vec, 0)
    vec_in[mine] = vec_out[p.c, mine]
    sc0.side_add(0)
    sc0.line(0, 0)
    sc0.line(0, 1)
    own_qo = sc0.final()
    dqo_ref[p.c] = own_qo
    qo_back = remote(dqo_ref.at[p.c], swap_grad, 5, p.sib)
    qo_back.start()
    most = remote(vec_out.at[p.c, pl.ds(0, 15)], vec_in.at[pl.ds(0, 15)], 4, p.sib)
    most.wait_recv()
    dvec_ref[...] = jnp.sum(vec_in[...], 0)
    qo_back.wait_recv()
    dqo_ref[1 - p.c] = swap_grad[...]

    swap_copy.wait_send()
    all_but_own.wait_send()
    share.wait_send()
    vec_swap.wait_send()
    most.wait_send()
    qo_back.wait_send()
    for g in (sm_g, qo_g, f1_g):
        g.drain()
    for s in (sc0, sc1, sc2):
        s.drain()


def swap(block, step, size):
    return lax.ppermute(block, "fsdp", [(i, i ^ step) for i in range(size)])


def pregather(block, F, r):
    step = 1
    while step < r:
        high = (lax.axis_index("fsdp") // step) % 2 == 1
        other = swap(block, step, F)
        block = jnp.concatenate([jnp.where(high, other, block), jnp.where(high, block, other)], 0)
        step *= 2
    return block


def postscatter(block, F, r):
    step = r // 2
    while step:
        high = (lax.axis_index("fsdp") // step) % 2 == 1
        middle = block.shape[0] // 2
        keep = jnp.where(high, block[middle:], block[:middle])
        send = jnp.where(high, block[:middle], block[middle:])
        block = keep + swap(send, step, F)
        step //= 2
    return block


def per_device(
    F,
    r,
    n,
    images,
    tissue,
    pair_index,
    text_embed,
    logit_scale,
    ln1_gain,
    ln1_bias,
    w_qkv,
    bias_qv,
    w_out,
    bias_out,
    ln2_gain,
    ln2_bias,
    w_fc1,
    bias_fc1,
    w_fc2,
    bias_fc2,
    cotangent,
):
    slots = images.shape[1]
    core = (lax.axis_index("fsdp") // r) % 2
    gather = lambda block: pregather(block, F, r)
    joined = gather(jnp.concatenate([w_qkv.T, w_out.T], 0).reshape(1, -1, D))
    rows_here = w_qkv.shape[1]
    q_t = joined[:, :rows_here].reshape(-1, D)
    o_t = joined[:, rows_here:].reshape(-1, D)

    def zeros(count):
        return jnp.zeros((count, D), BF)

    gap = QKV_ROWS - OUT_ROWS
    as_zero = jnp.concatenate([q_t, zeros(ROWS - QKV_ROWS), zeros(gap), o_t, zeros(OUT_ROWS)], 0)
    as_one = jnp.concatenate([zeros(QKV_ROWS), q_t, zeros(OUT_ROWS), o_t], 0)
    qo = jnp.where(core == 0, as_zero, as_one).reshape(2, ROWS, D)
    f1 = gather(w_fc1.T)
    f2 = gather(w_fc2)

    text_float = text_embed.astype(F32)
    text_unit = (text_float * lax.rsqrt(jnp.sum(text_float * text_float, -1, keepdims=True) + EPS)).astype(BF)
    vectors = jnp.stack([ln1_gain, ln1_bias, bias_out, ln2_gain, ln2_bias, bias_fc2], 1)
    vectors = gather(vectors)
    qv, first = gather(bias_qv), gather(bias_fc1)
    lanes = lambda v: jnp.pad(v, (0, 128 - v.shape[0])).reshape(1, 128)
    row0 = lanes(vectors[:, :5].T.reshape(-1))
    row1 = lanes(jnp.concatenate([vectors[:, 5], qv]))
    row2 = lanes(first)
    text_all = gather(text_unit).reshape(-1, 6, 128).transpose(1, 0, 2).reshape(-1, 128)
    pair = gather(pair_index)
    pair_rows = jnp.pad(jnp.stack([pair // 256, pair % 256], 1), ((0, 0), (0, 126))).astype(BF)
    small = jnp.concatenate([row0, row1, row2, text_all, pair_rows], 0)
    small_rows = -(-small.shape[0] // 16) * 16
    small = jnp.pad(small, ((0, small_rows - small.shape[0]), (0, 0)))

    def padded(tokens):
        return jnp.pad(tokens, ((0, 0), (0, PAD - slots), (0, 0))).reshape(TOK, D)

    mask = jnp.pad(tissue.astype(F32), ((0, 0), (0, PAD - slots))).reshape(TOK, 1)
    mask = jnp.broadcast_to(mask, (TOK, 128))
    text_in = jnp.pad(text_float, ((0, 8 - IMG), (0, 0)))
    scale = jnp.broadcast_to(logit_scale.reshape(1, 1), (8, 128))
    vmem = pl.BlockSpec(memory_space=pltpu.VMEM)
    shape = jax.ShapeDtypeStruct
    mix, res, loss, text_grad, dqo, df1, df2, dvec = pl.pallas_call(
        functools.partial(layer_kernel, F, r, n),
        out_shape=(
            shape((TOK, D), BF),
            shape((TOK, D), F32),
            shape((8, 128), F32),
            shape((8, D), F32),
            shape((2, ROWS, D), F32),
            shape((ROWS, D), F32),
            shape((ROWS, D), F32),
            shape((8, 128), F32),
        ),
        in_specs=[vmem] * 9,
        out_specs=(vmem,) * 8,
        scratch_shapes=[
            pltpu.VMEM((3, 2, 2, 4, 2, ROWS, D), BF),
            pltpu.VMEM((3, 2, 2, 4, 2, ROWS, D), BF),
            pltpu.VMEM((4, 4, 2, ROWS, D), BF),
            pltpu.VMEM((2, 3, ROWS, D), BF),
            pltpu.VMEM((2, 2, 4, 2, small_rows, 128), BF),
            pltpu.VMEM((ROWS, D), F32),
            pltpu.VMEM((TOK, D), BF),
            pltpu.VMEM((18, TOK, 128), BF),
            pltpu.VMEM((6, TOK, 128), BF),
            pltpu.VMEM((2 * IMG * 6, 1, PAD), F32),
            pltpu.VMEM((6, TOK, 128), BF),
            pltpu.VMEM((4, TOK, D), BF),
            pltpu.VMEM((4, TOK, D), BF),
            pltpu.VMEM((TOK, D), BF),
            pltpu.VMEM((max(TOK, IMG * n), D), F32),
            pltpu.VMEM((16, D), F32),
            pltpu.VMEM((16, D), F32),
            pltpu.VMEM((16, D), F32),
            pltpu.VMEM((8, D), F32),
            pltpu.VMEM((IMG * n, 128), F32),
            pltpu.VMEM((2, n // 2, 32, 128), BF),
            pltpu.VMEM((2, 16, 8, 128), F32),
            pltpu.VMEM((16, 8, 128), F32),
            pltpu.VMEM((16, 8, 128), F32),
            pltpu.SemaphoreType.DMA((4, 32)),
            pltpu.SemaphoreType.DMA((4, 32)),
            pltpu.SemaphoreType.DMA((3, 32)),
            pltpu.SemaphoreType.DMA((3, 32)),
            pltpu.SemaphoreType.DMA((16,)),
            pltpu.SemaphoreType.REGULAR((10,)),
        ],
        compiler_params=pltpu.CompilerParams(collective_id=0, has_side_effects=True, vmem_limit_bytes=VMEM_LIMIT),
    )(qo, f1, f2, small, padded(images), padded(cotangent), mask, text_in, scale)

    def tokens(rows):
        return rows.reshape(IMG, PAD, D)[:, :slots]

    scatter = lambda block: postscatter(block, F, r)
    chip = dqo.reshape(2 * ROWS, D)
    dq = jnp.where(core == 0, chip[:QKV_ROWS], chip[QKV_ROWS : 2 * QKV_ROWS])
    do = jnp.where(core == 0, chip[2 * QKV_ROWS : 2 * QKV_ROWS + OUT_ROWS], chip[2 * QKV_ROWS + OUT_ROWS :])
    thin = [dvec[0, 24 * k : 24 * k + 24] for k in range(5)] + [dvec[1, :24]]
    thin = [scatter(v) for v in thin]
    return (
        tokens(mix),
        tokens(res),
        loss[0, 0],
        text_grad[:IMG],
        thin[0],
        thin[1],
        scatter(dq).T,
        scatter(dvec[1, 24:72]),
        scatter(do).T,
        thin[2],
        thin[3],
        thin[4],
        scatter(df1).T,
        scatter(dvec[2, :96]),
        scatter(df2),
        thin[5],
    )


def solution(mesh):
    F = mesh.shape["fsdp"]
    n = mesh.shape["dp"] * F
    r = n // GROUPS
    both = ("dp", "fsdp")
    rows, columns = P(both), P(None, both)
    in_specs = (
        rows, rows, rows, rows, P(), rows, rows, columns, rows, columns, rows, rows, rows, columns, rows, rows, rows, rows
    )
    out_specs = (
        rows, rows, P(), rows, rows, rows, columns, rows, columns, rows, rows, rows, columns, rows, rows, rows
    )
    return jax.shard_map(
        functools.partial(per_device, F, r, n), mesh=mesh, in_specs=in_specs, out_specs=out_specs, check_vma=False
    )
```

time: 961 us -> 230 us (0.24)
  waiting for transfers between devices: 484 us -> 0 us
  blocking collectives: 247 us -> 0 us
  Pallas kernels: 0 us -> 201 us
  matrix products: 136 us -> 0 us
  other arithmetic: 31.5 us -> 6.91 us
  local copies, waits for them, and re-layouts: 36.5 us -> 17.6 us
  between operations: 20.1 us -> 1.71 us
    reduce_scatter x4 -> x0, waiting for transfers between devices: 368 us -> none  [the longest x1 142 us: per_device(): lax.psum_scatter(grad_totals[10], ('dp', 'fsdp'), scatter_dimension=0, ti...]
    pallas_call x0 -> x1, Pallas kernels: none -> 201 us  [per_device(): pl.pallas_call(functools.partial(layer_kernel, F, r, n), out_shape=(shape...]
    unnamed x4 -> x0, blocking collectives: 162 us -> none
    dot_general x58 -> x0, matrix products: 136 us -> none  [the longest x3 26.3 us: forward_block(): jnp.dot(second, w_fc1, preferred_element_type=jnp.float32)]
    all_gather x4 -> x0, waiting for transfers between devices: 114 us -> none  [the longest x1 55.1 us: per_device(): lax.all_gather(w_fc2, ('dp', 'fsdp'), axis=0, tiled=True)]
    all_gather x2 -> x0, blocking collectives: 84 us -> none  [the longest x1 42.8 us: per_device(): lax.all_gather(image_unit, ('dp', 'fsdp'), axis=0, tiled=True)]
    unnamed x317 -> x20, local copies, waits for them, and re-layouts: 26.9 us -> 1.48 us
    reduce_sum x22 -> x1, other arithmetic: 18.5 us -> 0.81 us  [per_device(): jnp.sum(text_float * text_float, -1, keepdims=True) + EPS]
  transfers between devices with their start and end apart: 8 -> 0, of which waited for: 6 -> 0; matrix products, arithmetic and copies ran while one was open for 10% -> 0% of each run, Pallas kernels for 0% -> 0%
where the time goes in v2:
time: 230 us; the launch traced here: 227 us
  Pallas kernels  201 us (87%)
  local copies, waits for them, and re-layouts  17.6 us (8%)
  other arithmetic  6.91 us (3%)
    pallas_call x1, Pallas kernels, per_device(): pl.pallas_call(functools.partial(layer_kernel, F, r, n), out_shape=(shape...  201 us
    slice x2, local copies, waits for them, and re-layouts, tokens(): return rows.reshape(IMG, PAD, D)[:, :slots]  5.14 us

profile of v2, /device:TPU:0, one launch (start us, length us, event | category | flops | bytes accessed | tf_op | source)
XLA Modules:
  0.0 227.1 jit_solution(14417212878048309235)
XLA Ops:
  0.6 0.0 copy-start
  1.4 0.7 fusion.8
  2.1 0.8 multiply_reduce_fusion
  3.0 0.7 convert_bitcast_fusion
  3.7 0.1 copy.35
  3.8 0.1 copy.36
  3.9 0.1 fusion.4
  3.9 0.7 stack.35
  4.7 0.1 reshape.92
  4.8 0.7 pad_bitcast_fusion
  5.4 0.6 broadcast_in_dim.23.scale_ref
  6.0 0.7 convert_element_type.27
  6.7 0.1 broadcast_in_dim.21
  6.8 0.8 multiply_convert_fusion
  7.6 0.2 concatenate.19
  7.8 0.6 pad.40.small_ref
  8.4 1.3 pad.44.text_ref
  9.7 0.9 maximum_bitcast_fusion
  10.7 0.0 copy-start.1
  10.8 0.9 maximum_select_fusion
  11.7 0.9 broadcast_in_dim.22.mask_ref
  12.5 0.0 copy-done
  12.5 1.0 pad.41
  13.5 0.0 copy-done.1
  13.5 1.0 pad.42
  14.5 200.9 %shard_map.297 = (bf16[624,768]{1,0:T(8,128)(2,1)}, f32[624,768]{1,0:T(8,128)}, f32[8,128]{1,0:T(8,128)}, f32[8,768]{1,0:T(8,128)}, f32[2,96,768]{2,1,0:T(8,128)...) custom-call(bf16[2,96,768]{2,1,0:T(8,128)(2,1)} %bitcast.61, bf16[96,768]{1,0:T(8,128)(2,1)} %bitcast.66, ...), custom_call_target="tpu_custom_call" | custom-call | tf_op jit(solution)/shard_map/pallas_call | solution.py:1206
  215.5 1.2 slice.58
  216.6 2.2 slice.74
  218.8 0.0 copy-start.6
  218.8 0.0 copy-start.5
  218.8 0.0 copy-start.2
  218.8 0.0 copy-start.4
  218.8 0.0 copy-start.3
  218.8 3.0 %slice.75 = f32[3,196,768]{2,1,0:T(8,128)} slice(f32[3,208,768]{2,1,0:T(8,128)} %bitcast.60), slice={[0:3], [0:196], [0:768]} | slice | bytes 3612672 | tf_op jit(solution)/shard_map/slice | solution.py:1256
  221.8 0.0 copy-done.6
  221.8 0.6 slice_bitcast_fusion.7
  222.4 0.5 slice_bitcast_fusion.3
  222.9 0.6 slice_bitcast_fusion.2
  223.5 0.0 copy-done.5
  223.5 0.6 slice.59
  224.1 0.0 copy-done.2
  224.1 0.6 fusion.1
  224.7 0.7 fusion
  225.5 0.0 copy-done.4
  225.5 0.7 copy.44
  226.2 0.0 copy-done.3
  226.2 0.7 copy.45
  (15 shorter events, 0.1 us)
Async XLA Ops:
  0.6 11.9 %copy-start = (bf16[3,196,768]{2,1,0:T(8,128)(2,1)S(1)}, bf16[3,196,768]{2,1,0:T(8,128)(2,1)}, u32[]{:S(2)}) copy-start(bf16[3,196,768]{2,1,0:T(8,128)(2,1)} %param.18) | copy-start | bytes 2709508
  10.7 2.9 %copy-start.1 = (bf16[3,196,768]{2,1,0:T(8,128)(2,1)S(1)}, bf16[3,196,768]{2,1,0:T(8,128)(2,1)}, u32[]{:S(2)}) copy-start(bf16[3,196,768]{2,1,0:T(8,128)(2,1)} %param.35) | copy-start | bytes 2709508
  218.8 3.0 %copy-start.6 = (f32[8,128]{1,0:T(8,128)S(1)}, f32[8,128]{1,0:T(8,128)}, u32[]{:S(2)}) copy-start(f32[8,128]{1,0:T(8,128)} %get-tuple-element.28) | copy-start | bytes 12292
  218.8 4.7 %copy-start.5 = (f32[8,768]{1,0:T(8,128)S(1)}, f32[8,768]{1,0:T(8,128)}, u32[]{:S(2)}) copy-start(f32[8,768]{1,0:T(8,128)} %get-tuple-element.27) | copy-start | bytes 73732
  218.8 5.3 %copy-start.2 = (f32[2,96,768]{2,1,0:T(8,128)S(1)}, f32[2,96,768]{2,1,0:T(8,128)}, u32[]{:S(2)}) copy-start(f32[2,96,768]{2,1,0:T(8,128)} %get-tuple-element.29) | copy-start | bytes 1769476
  218.8 6.6 %copy-start.4 = (f32[96,768]{1,0:T(8,128)S(1)}, f32[96,768]{1,0:T(8,128)}, u32[]{:S(2)}) copy-start(f32[96,768]{1,0:T(8,128)} %get-tuple-element.30) | copy-start | bytes 884740
  218.8 7.4 %copy-start.3 = (f32[96,768]{1,0:T(8,128)S(1)}, f32[96,768]{1,0:T(8,128)}, u32[]{:S(2)}) copy-start(f32[96,768]{1,0:T(8,128)} %get-tuple-element.72) | copy-start | bytes 884740

commit v3 on v2

--- a/solution.py
+++ b/solution.py
@@ -67,6 +67,26 @@
     def chip(p, y, x, z, c):
         return p.device((((y * 2 + x) * 4 + z) * 2 + c) * p.r + p.rho)
 
+    def column(p, zz):
+        return p.chip(p.y, p.x, zz, p.c)
+
+    def at_distance(p, h, fn):
+        if h == 0:
+            fn(p.z)
+            return
+
+        @pl.when(p.z + h <= 3)
+        def _():
+            fn(p.z + h)
+
+        @pl.when(p.z - h >= 0)
+        def _():
+            fn(p.z - h)
+
+    def for_others(p, fn):
+        for h in (1, 2, 3):
+            p.at_distance(h, fn)
+
     def in_plane(p, q):
         return p.device((lax.div(q, p.r) * 2 + p.c) * p.r + lax.rem(q, p.r))
 
@@ -91,20 +111,15 @@
 
 def enter(p):
     bar = pltpu.get_barrier_semaphore()
-    half = p.n // 2
-
-    def greet(i, carry):
-        pl.semaphore_signal(bar, inc=1, device_id=p.in_plane(lax.rem(p.plane + i, half)), device_id_type=MESH)
-        return carry
-
-    lax.fori_loop(1, half, greet, 0)
-    pl.semaphore_signal(bar, inc=1, device_id=p.sib, device_id_type=MESH)
-    pl.semaphore_wait(bar, half)
+    for device in (p.sib, p.fn, p.ln):
+        pl.semaphore_signal(bar, inc=1, device_id=device, device_id_type=MESH)
+    p.for_others(lambda zz: pl.semaphore_signal(bar, inc=1, device_id=p.column(zz), device_id_type=MESH))
+    pl.semaphore_wait(bar, 6)
 
 
 class Gather:
-    def __init__(s, p, held, send, recv):
-        s.p, s.held, s.send, s.recv = p, held, send, recv
+    def __init__(s, p, held, send, recv, line_first=False):
+        s.p, s.held, s.send, s.recv, s.line_first = p, held, send, recv, line_first
 
     def cp(s, at, ks, kr, dev):
         ref = s.held.at[at]
@@ -128,6 +143,12 @@
 
     def dn(s, zz, b):
         return s.cp((s.p.c, s.p.l, zz, s.f_of(b)), 9 + 2 * zz + b, 1 + 2 * zz + b, s.p.dn)
+
+    def cross(s, zz):
+        return s.cp((s.p.c, s.p.l, zz, s.p.f), 2 + 2 * zz, 2 + 2 * zz, s.p.fn)
+
+    def cross_in(s, zz):
+        return s.cp((s.p.c, s.p.l, zz, 1 - s.p.f), 2 + 2 * zz, 2 + 2 * zz, s.p.fn)
 
     def last(s, zz):
         return s.cp((s.p.c, s.p.l, zz), 17 + zz, 9 + zz, s.p.ln)
@@ -147,14 +168,15 @@
             s.first_in().wait_recv()
         else:
             s.first().start()
-
-        @pl.when(p.z < 3)
-        def _():
-            s.up(p.z, b).start()
-
-        @pl.when(p.z > 0)
-        def _():
-            s.dn(p.z, b).start()
+        if not (b and s.line_first):
+
+            @pl.when(p.z < 3)
+            def _():
+                s.up(p.z, b).start()
+
+            @pl.when(p.z > 0)
+            def _():
+                s.dn(p.z, b).start()
 
         if b:
             s.last(p.z).start()
@@ -163,31 +185,29 @@
     def line(s, h, b):
         p = s.p
 
-        @pl.when(p.z - h >= 0)
-        def _():
-            zz = p.z - h
-            s.up(zz, b).wait_recv()
-
-            @pl.when(p.z < 3)
-            def _():
-                s.up(zz, b).start()
-
+        def one(zz, copy, onward):
+            if b and s.line_first:
+                s.cross_in(zz).wait_recv()
+            else:
+                copy(zz, b).wait_recv()
+
+                @pl.when(onward)
+                def _():
+                    copy(zz, b).start()
+
+                if s.line_first:
+                    s.cross(zz).start()
             if b:
                 s.last(zz).start()
                 s.core(p.l, zz).start()
 
+        @pl.when(p.z - h >= 0)
+        def _():
+            one(p.z - h, s.up, p.z < 3)
+
         @pl.when(p.z + h <= 3)
         def _():
-            zz = p.z + h
-            s.dn(zz, b).wait_recv()
-
-            @pl.when(p.z > 0)
-            def _():
-                s.dn(zz, b).start()
-
-            if b:
-                s.last(zz).start()
-                s.core(p.l, zz).start()
+            one(p.z + h, s.dn, p.z > 0)
 
     def arrive(s, h):
         p = s.p
@@ -221,12 +241,20 @@
             @pl.when((p.z < 3) & (zz <= p.z))
             def _():
                 s.up(zz, 0).wait_send()
-                s.up(zz, 1).wait_send()
+                if not s.line_first:
+                    s.up(zz, 1).wait_send()
 
             @pl.when((p.z > 0) & (zz >= p.z))
             def _():
                 s.dn(zz, 0).wait_send()
-                s.dn(zz, 1).wait_send()
+                if not s.line_first:
+                    s.dn(zz, 1).wait_send()
+
+            if s.line_first:
+
+                @pl.when(zz != p.z)
+                def _():
+                    s.cross(zz).wait_send()
 
             s.last(zz).wait_send()
             for l in range(2):
@@ -234,8 +262,8 @@
 
 
 class Scatter:
-    def __init__(s, p, sums, room, ends, send, recv):
-        s.p, s.sums, s.room, s.ends, s.send, s.recv = p, sums, room, ends, send, recv
+    def __init__(s, p, sums, room, landing, send, recv, line_last=False):
+        s.p, s.sums, s.room, s.landing, s.send, s.recv, s.line_last = p, sums, room, landing, send, recv, line_last
 
     def cp(s, src, dst, ks, kr, dev):
         return pltpu.make_async_remote_copy(
@@ -258,13 +286,28 @@
         return s.cp(s.here(zz, b), s.room(3).at[zz, b], 7 + 2 * zz + b, 7 + 2 * zz + b, s.p.up)
 
     def up_end(s, zz, b):
-        return s.cp(s.here(zz, b), s.ends.at[b], 7 + 2 * zz + b, 15 + b, s.p.up)
+        return s.cp(s.here(zz, b), s.landing.at[b], 7 + 2 * zz + b, 15 + b, s.p.up)
 
     def down(s, zz, b):
         return s.cp(s.here(zz, b), s.room(3).at[zz, b], 15 + 2 * zz + b, 7 + 2 * zz + b, s.p.dn)
 
     def last_cp(s):
-        return s.cp(s.here(s.p.z, 0), s.ends.at[2], 0, 0, s.p.fn)
+        return s.cp(s.here(s.p.z, 0), s.landing.at[2], 0, 0, s.p.fn)
+
+    def cross_cp(s, zz):
+        return s.cp(s.here(zz, 0), s.room(3).at[zz, 0], 23 + zz, 17 + zz, s.p.fn)
+
+    def cross_send(s, h):
+        s.by_distance(h, lambda zz: s.cross_cp(zz).start())
+
+    def cross_add(s, h):
+        def one(zz):
+            s.cross_cp(zz).wait_recv()
+            s.add(zz, 1, s.room(3).at[zz, 0])
+            if h > 0:
+                s.straight(zz).start()
+
+        s.by_distance(h, one)
 
     def core_send(s, l):
         s.core_cp(l).start()
@@ -286,18 +329,7 @@
         total[...] = (total[...].astype(F32) + ref[...].astype(F32)).astype(BF)
 
     def by_distance(s, h, fn):
-        p = s.p
-        if h == 0:
-            fn(p.z)
-            return
-
-        @pl.when(p.z + h <= 3)
-        def _():
-            fn(p.z + h)
-
-        @pl.when(p.z - h >= 0)
-        def _():
-            fn(p.z - h)
+        s.p.at_distance(h, fn)
 
     def side_send(s):
         for h in (3, 2, 1, 0):
@@ -312,41 +344,49 @@
 
         s.by_distance(h, one)
 
-    def line(s, h, b):
+    def ends(s, h):
         p = s.p
-        if h > 0:
-
-            @pl.when(p.z + h <= 3)
+
+        @pl.when(p.z == 0)
+        def _():
+            for b in (0, 1):
+                (s.up_end if h == 1 else s.up_far)(p.z + h, b).start()
+
+        @pl.when(p.z == 3)
+        def _():
+            for b in (0, 1):
+                s.down(p.z - h, b).start()
+
+    def inner(s, h, upward):
+        p = s.p
+        if upward:
+
+            @pl.when((p.z == 1) | (p.z == 2) if h == 1 else p.z == 1)
             def _():
                 zz = p.z + h
-
-                @pl.when(p.z > 0)
-                def _():
+                for b in (0, 1):
                     s.up_far(zz, b).wait_recv()
                     s.add(zz, b, s.room(3).at[zz, b])
-
-                if h == 1:
-                    s.up_end(zz, b).start()
-                else:
-                    s.up_far(zz, b).start()
-
-            @pl.when(p.z - h >= 0)
+                    (s.up_end if h == 1 else s.up_far)(zz, b).start()
+
+        else:
+
+            @pl.when((p.z == 1) | (p.z == 2) if h == 1 else p.z == 2)
             def _():
                 zz = p.z - h
-
-                @pl.when(p.z < 3)
-                def _():
+                for b in (0, 1):
                     s.down(zz, b).wait_recv()
                     s.add(zz, b, s.room(3).at[zz, b])
-
-                s.down(zz, b).start()
-
-        else:
+                    s.down(zz, b).start()
+
+    def come(s):
+        p = s.p
+        for b in (0, 1):
 
             @pl.when(p.z > 0)
             def _():
                 s.up_end(p.z, b).wait_recv()
-                s.add(p.z, b, s.ends.at[b])
+                s.add(p.z, b, s.landing.at[b])
 
             @pl.when(p.z < 3)
             def _():
@@ -356,9 +396,24 @@
             if b == 0:
                 s.last_cp().start()
 
+    def straight(s, zz):
+        return s.cp(s.here(zz, 1), s.room(3).at[s.p.z, 1], 7 + zz, 7 + s.p.z, s.p.column(zz))
+
+    def straight_in(s, zz):
+        return s.cp(s.here(zz, 1), s.room(3).at[zz, 1], 7 + zz, 7 + zz, s.p.column(zz))
+
     def final(s):
+        p = s.p
+        if s.line_last:
+
+            def one(zz):
+                s.straight_in(zz).wait_recv()
+                s.add(p.z, 1, s.room(3).at[zz, 1])
+
+            p.for_others(one)
+            return s.here(p.z, 1)[...].astype(F32)
         s.last_cp().wait_recv()
-        return s.here(s.p.z, 1)[...].astype(F32) + s.ends[2].astype(F32)
+        return s.here(p.z, 1)[...].astype(F32) + s.landing[2].astype(F32)
 
     def drain(s):
         p = s.p
@@ -366,18 +421,27 @@
             s.core_cp(l).wait_send()
         for zz in range(4):
             s.side_cp(zz).wait_send()
-
-            @pl.when(zz > p.z)
-            def _():
-                s.up_far(zz, 0).wait_send()
-                s.up_far(zz, 1).wait_send()
-
-            @pl.when(zz < p.z)
-            def _():
-                s.down(zz, 0).wait_send()
-                s.down(zz, 1).wait_send()
-
-        s.last_cp().wait_send()
+            if s.line_last:
+                s.cross_cp(zz).wait_send()
+
+                @pl.when(zz != p.z)
+                def _():
+                    s.straight(zz).wait_send()
+
+            else:
+
+                @pl.when(zz > p.z)
+                def _():
+                    s.up_far(zz, 0).wait_send()
+                    s.up_far(zz, 1).wait_send()
+
+                @pl.when(zz < p.z)
+                def _():
+                    s.down(zz, 0).wait_send()
+                    s.down(zz, 1).wait_send()
+
+        if not s.line_last:
+            s.last_cp().wait_send()
 
 
 def qkv_runs(start, stop):
@@ -513,8 +577,8 @@
     total = IMG * n
     per_group = IMG * r
     small_rows = small.shape[4]
-    qo_g, f1_g, f2_g = (Gather(p, W.at[m], g_send.at[m], g_recv.at[m]) for m in range(3))
-    sm_g = Gather(p, small, g_send.at[3], g_recv.at[3])
+    qo_g, f1_g, f2_g = (Gather(p, W.at[m], g_send.at[m], g_recv.at[m], m == 0) for m in range(3))
+    sm_g = Gather(p, small, g_send.at[3], g_recv.at[3], True)
 
     def remote(src, dst, k, dev):
         return pltpu.make_async_remote_copy(
@@ -529,25 +593,26 @@
     swap_copy = remote(qo_ref.at[1 - p.c], G.at[0, 0, 0, 0, 0], 0, p.sib)
     swap_copy.start()
     sm_g.own(0)
-    f1_early = False
     swap_copy.wait_recv()
     W[0, p.c, p.l, p.z, p.f] = (qo_ref[p.c].astype(F32) + G[0, 0, 0, 0, 0].astype(F32)).astype(BF)
     qo_g.own(0)
+    f1_g.own(0)
     sm_g.own(1)
     qo_g.own(1)
-    sm_g.line(1, 0)
-    sm_g.line(1, 1)
-    sm_g.arrive(0)
-    qo_g.line(1, 0)
-    sm_g.line(2, 0)
-    sm_g.line(2, 1)
-    sm_g.arrive(1)
-    qo_g.line(1, 1)
-    qo_g.arrive(0)
-    sm_g.line(3, 0)
-    sm_g.line(3, 1)
-    sm_g.arrive(2)
-    sm_g.arrive(3)
+    for h in (1, 2, 3):
+        sm_g.line(h, 0)
+        qo_g.line(h, 0)
+        sm_g.line(h, 1)
+        qo_g.line(h, 1)
+        sm_g.arrive(h - 1)
+        if h == 1:
+            f1_g.own(1)
+        if h == 2:
+            f1_g.line(1, 0)
+        if h == 3:
+            f1_g.line(1, 1)
+            sm_g.arrive(3)
+        qo_g.arrive(h - 1)
     sm_g.finish()
 
 
@@ -578,14 +643,9 @@
         norm1[rows] = (normalized * vec[0:1] + vec[1:2]).astype(BF)
 
     by_rows(first_norm)
-    qo_g.line(2, 0)
-    qo_g.line(2, 1)
-    f1_g.own(0)
-    qo_g.arrive(1)
-    f1_g.own(1)
-    qo_g.line(3, 0)
-    qo_g.line(3, 1)
-    qo_g.arrive(2)
+    f1_g.arrive(0)
+    f1_g.line(2, 0)
+    f2_g.own(0)
     qo_g.arrive(3)
     qo_g.finish()
 
@@ -598,16 +658,13 @@
         part = part.astype(BF)
         qkv[2 * j] = part[:, :128]
         qkv[2 * j + 1] = part[:, 128:]
-        if j == 2:
-            f1_g.line(1, 0)
-            f1_g.line(1, 1)
-            f1_g.arrive(0)
-        if j == 6:
-            f1_g.line(2, 0)
+        if j == 4:
             f1_g.line(2, 1)
-            f2_g.own(0)
             f1_g.arrive(1)
             f2_g.own(1)
+
+    def image_rows(i):
+        return pl.ds(pl.multiple_of(i * PAD, 16), PAD)
 
     low = iota((1, 128), 1) < 64
 
@@ -619,36 +676,42 @@
         rows = pl.ds(pl.multiple_of(i * PAD, 16), PAD)
         return rows, qkv[pair, rows], qkv[6 + pair, rows], qkv[12 + pair, rows]
 
+    PAIRS = 2
+
     def attend(it, carry):
-        i, pair = lax.div(it, 6), lax.rem(it, 6)
-        rows, q, k, v = head_pair(i, pair)
-        v_t = v.T
-        bars = jnp.concatenate([jnp.where(mask_ref[rows] > 0, 0.0, -1e30)] * 2, 1)[:, :PAD]
-        parts = []
-        for h, k_h in enumerate(halves(k * jnp.asarray(0.125, BF))):
-            scores = dot_nt(k_h, q) + bars
-            top = jnp.max(scores, 0, keepdims=True)
-            terms = jnp.exp(scores - top)
-            amount = jnp.sum(terms, 0, keepdims=True)
-            lse[it * 2 + h] = top + jnp.log(amount)
-            parts.append(dot(v_t[64 * h : 64 * h + 64], terms.astype(BF)) * (1.0 / amount))
-        att[pair, rows] = jnp.concatenate(parts, 0).T.astype(BF)
+        i, first = lax.div(it, 6 // PAIRS), lax.rem(it, 6 // PAIRS) * PAIRS
+        bars = jnp.concatenate([jnp.where(mask_ref[image_rows(i)] > 0, 0.0, -1e30)] * 2, 1)[:, :PAD]
+        results = []
+        for step in range(PAIRS):
+            rows, q, k, v = head_pair(i, first + step)
+            v_t = v.T
+            parts = []
+            for h, k_h in enumerate(halves(k * jnp.asarray(0.125, BF))):
+                scores = dot_nt(k_h, q) + bars
+                top = jnp.max(scores, 0, keepdims=True)
+                terms = jnp.exp(scores - top)
+                amount = jnp.sum(terms, 0, keepdims=True)
+                lse[(i * 6 + first + step) * 2 + h] = top + jnp.log(amount)
+                parts.append(dot(v_t[64 * h : 64 * h + 64], terms.astype(BF)) * (1.0 / amount))
+            results.append(jnp.concatenate(parts, 0).T.astype(BF))
+        for step in range(PAIRS):
+            att[first + step, rows] = results[step]
         return carry
 
-    lax.fori_loop(0, 4, attend, 0)
+    lax.fori_loop(0, 3, attend, 0)
     f1_g.line(3, 0)
+    f2_g.line(1, 0)
     f1_g.line(3, 1)
     f1_g.arrive(2)
-    lax.fori_loop(4, 8, attend, 0)
+    lax.fori_loop(3, 5, attend, 0)
+    f2_g.line(1, 1)
     f1_g.arrive(3)
-    f2_g.line(1, 0)
-    f2_g.line(1, 1)
     f2_g.arrive(0)
-    lax.fori_loop(8, 14, attend, 0)
+    lax.fori_loop(5, 7, attend, 0)
     f2_g.line(2, 0)
     f2_g.line(2, 1)
     f2_g.arrive(1)
-    lax.fori_loop(14, 18, attend, 0)
+    lax.fori_loop(7, 9, attend, 0)
 
     attended = slabs(att, 0, 6)
     for j in range(3):
@@ -664,9 +727,6 @@
 
     by_rows(second_norm)
     f1_g.finish()
-
-    def image_rows(i):
-        return pl.ds(pl.multiple_of(i * PAD, 16), PAD)
 
     def expand(it, carry):
         q, rows = lax.div(it, IMG), image_rows(lax.rem(it, IMG))
@@ -850,7 +910,7 @@
     tg_ref[...] = unit_grad(grad_text, text_rows, text_inverse)
 
     sc0, sc1, sc2 = (
-        Scatter(p, G.at[m], area, ends.at[1 if m == 1 else 0], s_send.at[m], s_recv.at[m])
+        Scatter(p, G.at[m], area, ends.at[1 if m == 1 else 0], s_send.at[m], s_recv.at[m], m == 0)
         for m, area in (
             (0, lambda k: room.at[k]),
             (1, lambda k: W.at[2, k // 2, k % 2] if isinstance(k, int) else W.at[2, 0, k]),
@@ -881,83 +941,54 @@
         weight_grad(2, at, act[2 * at[0] + at[1]], grad2[...])
         if step == 0:
             sc2.core_send(1 - p.f)
-        if step == 1:
+        if step == 2:
+            sc2.core_send(p.f)
+    for q in range(4):
+        for part in range(2):
+            lanes = slice(384 * part, 384 * part + 384)
+            value = dot_nt(grad2[...], W[2, q // 2, q % 2, 2 * part : 2 * part + 2].reshape(384, D)) * slope[q, :, lanes].astype(F32)
+            value = value.astype(BF)
+            slope[q, :, lanes] = value
+            vec_grad[8 + q : 9 + q, lanes] = jnp.sum(value.astype(F32), 0, keepdims=True)
+        if q == 0:
             sc2.core_add(1 - p.l)
             sc2.side_send()
-        if step == 2:
-            sc2.core_send(p.f)
-    sc2.core_add(p.l)
+        if q == 1:
+            sc2.core_add(p.l)
     sc2.side_add(3)
-    sc2.line(3, 0)
-    sc2.line(3, 1)
-    for q in range(4):
-
-        def back(i, carry, q=q):
-            rows = image_rows(i)
-            value = dot_nt(grad2[rows], W[2, q // 2, q % 2].reshape(D, D)) * slope[q, rows].astype(F32)
-            value = value.astype(BF)
-            slope[q, rows] = value
-            vec_grad[8 + q : 9 + q] += jnp.sum(value.astype(F32), 0, keepdims=True)
-            return carry
-
-        lax.fori_loop(0, IMG, back, 0)
-        if q == 1:
-            sc2.side_add(2)
-            sc2.line(2, 0)
-            sc2.line(2, 1)
+    sc2.ends(3)
     f2_g.drain()
-    line_up, line_down = p.z < 3, p.z > 0
 
     def give(k):
-        pl.semaphore_signal(credit.at[k], inc=1, device_id=p.sib, device_id_type=MESH)
-        pl.semaphore_signal(credit.at[k + 1], inc=1, device_id=p.ln, device_id_type=MESH)
-        pl.semaphore_signal(credit.at[k + 4], inc=1, device_id=p.fn, device_id_type=MESH)
-
-        @pl.when(line_down)
-        def _():
-            pl.semaphore_signal(credit.at[k + 2], inc=1, device_id=p.dn, device_id_type=MESH)
-
-        @pl.when(line_up)
-        def _():
-            pl.semaphore_signal(credit.at[k + 3], inc=1, device_id=p.up, device_id_type=MESH)
-
-    def take_line(k):
-        pl.semaphore_wait(credit.at[k + 4], 1)
-
-        @pl.when(line_up)
-        def _():
-            pl.semaphore_wait(credit.at[k + 2], 1)
-
-        @pl.when(line_down)
-        def _():
-            pl.semaphore_wait(credit.at[k + 3], 1)
+        for at, device in ((0, p.sib), (1, p.ln), (2, p.fn)):
+            pl.semaphore_signal(credit.at[k, at], inc=1, device_id=device, device_id_type=MESH)
+        p.for_others(lambda zz: pl.semaphore_signal(credit.at[k, 3 + p.z], inc=1, device_id=p.column(zz), device_id_type=MESH))
+
+    def take(k, *which):
+        for at in which:
+            pl.semaphore_wait(credit.at[k, at], 1)
+
+    def take_column(k):
+        p.for_others(lambda zz: pl.semaphore_wait(credit.at[k, 3 + zz], 1))
 
     give(0)
     for step, at in enumerate(order):
         weight_grad(1, at, slope[2 * at[0] + at[1]], slabs(sec, 0, 6))
         if step == 0:
-            pl.semaphore_wait(credit.at[0], 1)
+            take(0, 0)
             sc1.core_send(1 - p.f)
-            sc2.side_add(1)
-            sc2.line(1, 0)
-            sc2.line(1, 1)
-        if step == 1:
-            sc1.core_add(1 - p.l)
-            pl.semaphore_wait(credit.at[1], 1)
-            sc1.side_send()
         if step == 2:
             sc1.core_send(p.f)
+            sc2.side_add(2)
+            sc2.ends(2)
+    contract(slope, 1)
+    sc1.core_add(1 - p.l)
+    take(0, 1)
+    sc1.side_send()
     sc1.core_add(p.l)
+    sc2.side_add(1)
+    sc2.ends(1)
     sc2.side_add(0)
-    sc2.line(0, 0)
-    sc2.line(0, 1)
-    take_line(0)
-    sc1.side_add(3)
-    sc1.line(3, 0)
-    sc1.line(3, 1)
-    contract(slope, 1)
-    df2_ref[...] = sc2.final()
-    give(5)
 
     def second_back(i, rows):
         grad = temp[rows]
@@ -971,9 +1002,8 @@
         vec_grad[2:3] += jnp.sum(rounded.astype(F32), 0, keepdims=True)
 
     by_rows(second_back)
-    sc1.side_add(2)
-    sc1.line(2, 0)
-    sc1.line(2, 1)
+    sc2.inner(2, True)
+    sc2.inner(2, False)
     attended = slabs(att, 0, 6)
     for j in range(3):
         lanes = slice(256 * j, 256 * j + 256)
@@ -985,55 +1015,62 @@
         sec[2 * j + 1] = part[:, 128:]
 
     def attend_back(it, carry):
-        i, pair = lax.div(it, 6), lax.rem(it, 6)
-        rows, q, k, v = head_pair(i, pair)
-        grad_out = sec[pair, rows]
-        q, k = q * jnp.asarray(0.125, BF), k * jnp.asarray(0.125, BF)
-        k_t = k.T
-        bars = jnp.concatenate([jnp.where(mask_ref[rows] > 0, 0.0, -1e30)] * 2, 1)[:, :PAD]
-        q_halves, out_halves, v_halves = halves(q), halves(grad_out), halves(v)
-        plain_q = qkv[pair, rows]
-        grad_v, grad_k, grad_q = 0.0, 0.0, []
-        for h, k_h in enumerate(halves(k)):
-            scores = dot_nt(k_h, plain_q) + bars
-            probs = jnp.exp(scores - lse[it * 2 + h])
-            grad_v = grad_v + dot(probs.astype(BF), out_halves[h])
-            grad_probs = dot_nt(v_halves[h], grad_out)
-            grad_scores = (probs * (grad_probs - jnp.sum(grad_probs * probs, 0, keepdims=True))).astype(BF)
-            grad_k = grad_k + dot(grad_scores, q_halves[h])
-            grad_q.append(dot(k_t[64 * h : 64 * h + 64], grad_scores))
-        qkv[pair, rows] = jnp.concatenate(grad_q, 0).T.astype(BF)
-        qkv[6 + pair, rows] = grad_k.astype(BF)
-        qkv[12 + pair, rows] = grad_v.astype(BF)
+        i, first = lax.div(it, 6 // PAIRS), lax.rem(it, 6 // PAIRS) * PAIRS
+        bars = jnp.concatenate([jnp.where(mask_ref[image_rows(i)] > 0, 0.0, -1e30)] * 2, 1)[:, :PAD]
+        results = []
+        for step in range(PAIRS):
+            rows, plain_q, k, v = head_pair(i, first + step)
+            grad_out = sec[first + step, rows]
+            q, k = plain_q * jnp.asarray(0.125, BF), k * jnp.asarray(0.125, BF)
+            k_t = k.T
+            q_halves, out_halves, v_halves = halves(q), halves(grad_out), halves(v)
+            grad_v, grad_k, grad_q = 0.0, 0.0, []
+            for h, k_h in enumerate(halves(k)):
+                scores = dot_nt(k_h, plain_q) + bars
+                probs = jnp.exp(scores - lse[(i * 6 + first + step) * 2 + h])
+                grad_v = grad_v + dot(probs.astype(BF), out_halves[h])
+                grad_probs = dot_nt(v_halves[h], grad_out)
+                grad_scores = (probs * (grad_probs - jnp.sum(grad_probs * probs, 0, keepdims=True))).astype(BF)
+                grad_k = grad_k + dot(grad_scores, q_halves[h])
+                grad_q.append(dot(k_t[64 * h : 64 * h + 64], grad_scores))
+            results.append((jnp.concatenate(grad_q, 0).T.astype(BF), grad_k.astype(BF), grad_v.astype(BF)))
+        for step in range(PAIRS):
+            for which in range(3):
+                qkv[6 * which + first + step, rows] = results[step][which]
         return carry
 
-    lax.fori_loop(0, 6, attend_back, 0)
+    take(0, 2)
+    take_column(0)
+    lax.fori_loop(0, 2, attend_back, 0)
+    sc1.side_add(3)
+    sc1.ends(3)
+    lax.fori_loop(2, 4, attend_back, 0)
+    sc2.inner(1, True)
+    sc2.inner(1, False)
+    sc1.side_add(2)
+    sc1.ends(2)
+    lax.fori_loop(4, 6, attend_back, 0)
     sc1.side_add(1)
-    sc1.line(1, 0)
-    sc1.line(1, 1)
-    lax.fori_loop(6, 14, attend_back, 0)
+    sc1.ends(1)
     sc1.side_add(0)
-    sc1.line(0, 0)
-    sc1.line(0, 1)
-    lax.fori_loop(14, 18, attend_back, 0)
+    lax.fori_loop(6, 9, attend_back, 0)
+    sc2.come()
     for j in range(9):
         left = slabs(qkv, 2 * j, 2)
         store_runs(G.at[0], qkv_runs(256 * j, 256 * j + 256), dot(left.T, norm1[...]).astype(BF))
         if j < 3 or j >= 6:
             row, lanes = (6, slice(256 * j, 256 * j + 256)) if j < 3 else (7, slice(256 * (j - 6), 256 * (j - 6) + 256))
             vec_grad[row : row + 1, lanes] = jnp.sum(left.astype(F32), 0, keepdims=True)
-    pl.semaphore_wait(credit.at[5], 1)
+    sc1.inner(2, True)
+    sc1.inner(2, False)
+    df2_ref[...] = sc2.final()
+    give(1)
+    take(1, 0)
     sc0.core_send(1 - p.f)
     sc0.core_send(p.f)
     sc0.core_add(1 - p.l)
-    pl.semaphore_wait(credit.at[6], 1)
+    take(1, 1)
     sc0.side_send()
-    sc0.core_add(p.l)
-    df1_ref[...] = sc1.final()
-    take_line(5)
-    sc0.side_add(3)
-    sc0.line(3, 0)
-    sc0.line(3, 1)
 
     def contract_joined(i, carry):
         rows = image_rows(i)
@@ -1044,9 +1081,11 @@
         return carry
 
     lax.fori_loop(0, IMG, contract_joined, 0)
-    sc0.side_add(2)
-    sc0.line(2, 0)
-    sc0.line(2, 1)
+    sc0.core_add(p.l)
+    sc1.inner(1, True)
+    sc1.inner(1, False)
+    take(1, 2)
+    take_column(1)
 
     def first_back(i, rows):
         grad = temp[rows]
@@ -1056,24 +1095,45 @@
         vec_grad[1:2] += jnp.sum(grad, 0, keepdims=True)
 
     by_rows(first_back)
-    sc0.side_add(1)
-    sc0.line(1, 0)
-    sc0.line(1, 1)
+    for h in (3, 2):
+        sc0.side_add(h)
+        sc0.cross_send(h)
+
+    def two_parts(value):
+        high = value.astype(BF)
+        return jnp.concatenate([high, (value - high.astype(F32)).astype(BF)], 0)
 
     @pl.when(p.index >= 0)
     def _():
-      outgoing = jnp.zeros((GROUPS * 8, 128), F32)
-      for k in range(3):
-          rows_k = jnp.zeros((GROUPS, 128), F32)
-          for row, (kk, offset, width, base) in enumerate(table):
-              if kk == k:
-                  mask, places = spread(k, offset, width, base)
-                  rows_k = rows_k + dot_exact(mask * vec_grad[row : row + 1], places, ((1,), (1,)))
-          at = jnp.where(iota((GROUPS * 8, GROUPS), 0) == 8 * iota((GROUPS * 8, GROUPS), 1) + k, 1.0, 0.0)
-          outgoing = outgoing + dot_exact(at, rows_k, ((1,), (0,)))
-      vec_out[...] = outgoing.reshape(2, 16, 8, 128)
+        lines = []
+        for k in range(3):
+            line = jnp.zeros((2 * GROUPS, 128), F32)
+            for row, (kk, offset, width, base) in enumerate(table):
+                if kk == k:
+                    mask, places = spread(k, offset, width, base)
+                    line = line + dot_nt(two_parts(mask * vec_grad[row : row + 1]), places.astype(BF))
+            lines.append(line[:GROUPS] + line[GROUPS:])
+        shape = (GROUPS * 8, 2 * 3 * GROUPS)
+        source, target = iota(shape, 1), iota(shape, 0)
+        source = jnp.where(source >= 3 * GROUPS, source - 3 * GROUPS, source)
+        k = jnp.where(source >= GROUPS, 1, 0) + jnp.where(source >= 2 * GROUPS, 1, 0)
+        at = jnp.where(target == 8 * (source - GROUPS * k) + k, 1.0, 0.0).astype(BF)
+        vec_out[...] = dot(at, two_parts(jnp.concatenate(lines, 0))).reshape(2, 16, 8, 128)
+
     vec_swap = remote(vec_out.at[1 - p.c], vec_core, 3, p.sib)
     vec_swap.start()
+    for h in (1, 0):
+        sc0.side_add(h)
+        sc0.cross_send(h)
+    sc0.cross_add(3)
+    sc1.come()
+    for h in (2, 1, 0):
+        sc0.cross_add(h)
+    df1_ref[...] = sc1.final()
+    own_qo = sc0.final()
+    dqo_ref[p.c] = own_qo
+    qo_back = remote(dqo_ref.at[p.c], swap_grad, 5, p.sib)
+    qo_back.start()
     vec_swap.wait_recv()
     vec_out[p.c] += vec_core[...]
     mine = (p.l * 4 + p.z) * 2 + p.f
@@ -1086,13 +1146,6 @@
 
     lax.fori_loop(1, 16, push_vec, 0)
     vec_in[mine] = vec_out[p.c, mine]
-    sc0.side_add(0)
-    sc0.line(0, 0)
-    sc0.line(0, 1)
-    own_qo = sc0.final()
-    dqo_ref[p.c] = own_qo
-    qo_back = remote(dqo_ref.at[p.c], swap_grad, 5, p.sib)
-    qo_back.start()
     most = remote(vec_out.at[p.c, pl.ds(0, 15)], vec_in.at[pl.ds(0, 15)], 4, p.sib)
     most.wait_recv()
     dvec_ref[...] = jnp.sum(vec_in[...], 0)
@@ -1247,7 +1300,7 @@
             pltpu.SemaphoreType.DMA((3, 32)),
             pltpu.SemaphoreType.DMA((3, 32)),
             pltpu.SemaphoreType.DMA((16,)),
-            pltpu.SemaphoreType.REGULAR((10,)),
+            pltpu.SemaphoreType.REGULAR((2, 8)),
         ],
         compiler_params=pltpu.CompilerParams(collective_id=0, has_side_effects=True, vmem_limit_bytes=VMEM_LIMIT),
     )(qo, f1, f2, small, padded(images), padded(cotangent), mask, text_in, scale)

time: 230 us -> 208 us (0.904)
  Pallas kernels: 201 us -> 179 us
    pallas_call x1, Pallas kernels: 201 us -> 179 us  [per_device(): pl.pallas_call(functools.partial(layer_kernel, F, r, n), out_shape=(shape...]
where the time goes in v3:
time: 208 us; the launch traced here: 205 us
  Pallas kernels  179 us (86%)
  local copies, waits for them, and re-layouts  17.6 us (8%)
  other arithmetic  6.91 us (3%)
    pallas_call x1, Pallas kernels, per_device(): pl.pallas_call(functools.partial(layer_kernel, F, r, n), out_shape=(shape...  179 us
    slice x2, local copies, waits for them, and re-layouts, tokens(): return rows.reshape(IMG, PAD, D)[:, :slots]  5.14 us

profile of v3, /device:TPU:0, one launch (start us, length us, event | category | flops | bytes accessed | tf_op | source)
XLA Modules:
  0.0 204.7 jit_solution(18416789247869491521)
XLA Ops:
  0.6 0.0 copy-start
  1.4 0.7 fusion.8
  2.1 0.8 multiply_reduce_fusion
  3.0 0.7 convert_bitcast_fusion
  3.7 0.1 copy.35
  3.8 0.1 copy.36
  3.9 0.1 fusion.4
  3.9 0.7 stack.35
  4.7 0.1 reshape.92
  4.8 0.7 pad_bitcast_fusion
  5.4 0.6 broadcast_in_dim.23.scale_ref
  6.0 0.7 convert_element_type.27
  6.7 0.1 broadcast_in_dim.21
  6.8 0.8 multiply_convert_fusion
  7.6 0.2 concatenate.19
  7.8 0.6 pad.40.small_ref
  8.4 1.3 pad.44.text_ref
  9.7 0.9 maximum_bitcast_fusion
  10.7 0.0 copy-start.1
  10.8 0.9 maximum_select_fusion
  11.7 0.9 broadcast_in_dim.22.mask_ref
  12.5 0.0 copy-done
  12.5 1.0 pad.41
  13.5 0.0 copy-done.1
  13.5 1.0 pad.42
  14.5 178.5 %shard_map.297 = (bf16[624,768]{1,0:T(8,128)(2,1)}, f32[624,768]{1,0:T(8,128)}, f32[8,128]{1,0:T(8,128)}, f32[8,768]{1,0:T(8,128)}, f32[2,96,768]{2,1,0:T(8,128)...) custom-call(bf16[2,96,768]{2,1,0:T(8,128)(2,1)} %bitcast.61, bf16[96,768]{1,0:T(8,128)(2,1)} %bitcast.66, ...), custom_call_target="tpu_custom_call" | custom-call | tf_op jit(solution)/shard_map/pallas_call | solution.py:1259
  193.1 1.2 slice.58
  194.3 2.2 %slice.74 = bf16[3,196,768]{2,1,0:T(8,128)(2,1)} slice(bf16[3,208,768]{2,1,0:T(8,128)(2,1)} %bitcast.62), slice={[0:3], [0:196], [0:768]} | slice | bytes 1806336 | tf_op jit(solution)/shard_map/slice | solution.py:1309
  196.4 0.0 copy-start.6
  196.4 0.0 copy-start.5
  196.4 0.0 copy-start.2
  196.5 0.0 copy-start.4
  196.5 0.0 copy-start.3
  196.5 3.0 %slice.75 = f32[3,196,768]{2,1,0:T(8,128)} slice(f32[3,208,768]{2,1,0:T(8,128)} %bitcast.60), slice={[0:3], [0:196], [0:768]} | slice | bytes 3612672 | tf_op jit(solution)/shard_map/slice | solution.py:1309
  199.4 0.0 copy-done.6
  199.4 0.6 slice_bitcast_fusion.7
  200.0 0.5 slice_bitcast_fusion.3
  200.5 0.6 slice_bitcast_fusion.2
  201.1 0.0 copy-done.5
  201.1 0.6 slice.59
  201.7 0.0 copy-done.2
  201.7 0.6 fusion.1
  202.4 0.7 fusion
  203.1 0.0 copy-done.4
  203.1 0.7 copy.44
  203.8 0.0 copy-done.3
  203.8 0.7 copy.45
  (15 shorter events, 0.1 us)
Async XLA Ops:
  0.6 11.9 %copy-start = (bf16[3,196,768]{2,1,0:T(8,128)(2,1)S(1)}, bf16[3,196,768]{2,1,0:T(8,128)(2,1)}, u32[]{:S(2)}) copy-start(bf16[3,196,768]{2,1,0:T(8,128)(2,1)} %param.18) | copy-start | bytes 2709508
  10.7 2.9 %copy-start.1 = (bf16[3,196,768]{2,1,0:T(8,128)(2,1)S(1)}, bf16[3,196,768]{2,1,0:T(8,128)(2,1)}, u32[]{:S(2)}) copy-start(bf16[3,196,768]{2,1,0:T(8,128)(2,1)} %param.35) | copy-start | bytes 2709508
  196.4 3.0 %copy-start.6 = (f32[8,128]{1,0:T(8,128)S(1)}, f32[8,128]{1,0:T(8,128)}, u32[]{:S(2)}) copy-start(f32[8,128]{1,0:T(8,128)} %get-tuple-element.28) | copy-start | bytes 12292
  196.4 4.7 %copy-start.5 = (f32[8,768]{1,0:T(8,128)S(1)}, f32[8,768]{1,0:T(8,128)}, u32[]{:S(2)}) copy-start(f32[8,768]{1,0:T(8,128)} %get-tuple-element.27) | copy-start | bytes 73732
  196.4 5.3 %copy-start.2 = (f32[2,96,768]{2,1,0:T(8,128)S(1)}, f32[2,96,768]{2,1,0:T(8,128)}, u32[]{:S(2)}) copy-start(f32[2,96,768]{2,1,0:T(8,128)} %get-tuple-element.29) | copy-start | bytes 1769476
  196.5 6.6 %copy-start.4 = (f32[96,768]{1,0:T(8,128)S(1)}, f32[96,768]{1,0:T(8,128)}, u32[]{:S(2)}) copy-start(f32[96,768]{1,0:T(8,128)} %get-tuple-element.30) | copy-start | bytes 884740
  196.5 7.4 %copy-start.3 = (f32[96,768]{1,0:T(8,128)S(1)}, f32[96,768]{1,0:T(8,128)}, u32[]{:S(2)}) copy-start(f32[96,768]{1,0:T(8,128)} %get-tuple-element.72) | copy-start | bytes 884740
